TPU v7x, 32 devices: a whole 2x2x4 slice. The times are simulated.
32 devices in a mesh: ctx: 4 (over y, x), head: 8 (over z, core).
Axes of the slice: x: 2, y: 2, z: 4, core: 2. Of those that a mesh axis runs over, the one named last changes fastest.
Arguments:
- tokens: bfloat16 [2048, 8192], P('ctx'), may hold values from -6 to 6
- w_zx: bfloat16 [8192, 2, 8192], P('ctx', None, 'head'), may hold values from -0.0625 to 0.0625
- zx_scale: float32 [2, 8192], P(None, 'head'), may hold values from 0.5 to 2
- w_bc: bfloat16 [8192, 8, 512], P('ctx'), may hold values from -0.0625 to 0.0625
- bc_scale: float32 [8, 512], replicated, may hold values from 0.5 to 2
- w_dt: bfloat16 [8192, 128], P('ctx', 'head'), may hold values from -0.0625 to 0.0625
- conv_x: float32 [5, 8192], P(None, 'head'), may hold values from -3 to 3
- conv_bc: float32 [5, 8, 512], replicated, may hold values from -3 to 3
- tail_x: bfloat16 [3, 8192], P(None, 'head'), may hold values from -6 to 6
- tail_bc: bfloat16 [3, 8, 512], replicated, may hold values from -6 to 6
- head_params: float32 [3, 128], P(None, 'head'), may hold values from -12 to 2, as said below
- init_state: float32 [128, 64, 256], P('head'), may hold values from -1.5 to 1.5
- norm_gain: float32 [8192], P('head'), may hold values from 0.5 to 1.5
Outputs:
- mixed: bfloat16 [2048, 8192], P('ctx', 'head')
Inputs may be any that keep to these rules, and one draw needn't show every extreme that they name: `head_params`: row 0 lies in -3.5 to -2.5 and row 2 in 0.5 to 1.5.
All inputs are finite; a program needn't handle non-finite values.
Results may differ from a plain program's by a relative error of at most 0.0052.
Values may be sent and summed in bfloat16 or wider, within the bound.
No kernel may reach another device: no remote copies, remote signals or barrier semaphores. Data moves between devices by JAX's collectives and lax.ppermute only.
A program may use at most 256 MiB of HBM per device.

v0:
```python
import functools
import jax
import jax.numpy as jnp
from jax import lax
from jax.experimental import pallas as pl
from jax.experimental.pallas import tpu as pltpu
from jax.sharding import PartitionSpec as P

H = 128
P_SIZE = 64
N = 256
G = 8
K = 4
SLOTS = 4
LANES = 128
EDGE = 16
LOG_ROWS = 16
LOG_PARTS = 3
EARLY = 2
MIB = 1 << 20
MAIN_MIB = 32
SCALE = 64
BF16 = jnp.bfloat16
F32 = jnp.float32
VMEM = pl.BlockSpec(memory_space=pltpu.VMEM)
SMEM = pl.BlockSpec(memory_space=pltpu.SMEM)
ANY = pl.BlockSpec(memory_space=pl.ANY)


def shape_of(shape, dtype):
    return jax.ShapeDtypeStruct(shape, dtype)


def params(mib):
    return pltpu.CompilerParams(vmem_limit_bytes=mib * MIB)


def cost(flops, moved, transcendentals=0):
    return pl.CostEstimate(
        flops=int(flops) // SCALE, bytes_accessed=int(moved) // SCALE, transcendentals=int(transcendentals) // SCALE
    )


def chained(values, after):
    return lax.optimization_barrier((*values, after))[: len(values)]


def passed_along(x, axis, by):
    length = lax.axis_size(axis)
    pairs = [(i, i + by) for i in range(length) if 0 <= i + by < length]
    return lax.ppermute(x, axis, pairs)


def swapped(x, axis, by):
    length = lax.axis_size(axis)
    return lax.ppermute(x, axis, [(i, i ^ by) for i in range(length)])


def pick_group(values, group_index, axis_index):
    return lax.dynamic_index_in_dim(values, group_index, axis_index, keepdims=False)


def dot32(a, b):
    return jnp.dot(a, b, preferred_element_type=F32)


def silu(v):
    return v / (1.0 + jnp.exp(-v))


def pack_kernel(n, place_ref, *refs):
    blocks, tails, dt_ref, outs = refs[: n - 1], refs[n - 1 : 2 * n - 2], refs[2 * n - 2], refs[2 * n - 1 :]
    part, edge = blocks[0].shape[0], tails[0].shape[0]
    for block, tail, out in zip(blocks, tails, outs):
        out[:part] = block[...]
        out[part : part + edge] = tail[...]
        out[part + edge :] = dt_ref[...]


def pack(place, tokens, dt_t, n):
    dt_rows, depth = dt_t.shape
    part = tokens.shape[0] // SLOTS
    height = part + EDGE + dt_rows
    last = tokens.shape[0] // EDGE - 1
    return pl.pallas_call(
        functools.partial(pack_kernel, n),
        grid_spec=pltpu.PrefetchScalarGridSpec(
            num_scalar_prefetch=1,
            grid=(1,),
            in_specs=[
                pl.BlockSpec((part, depth), lambda i, place, j=j: (place[0], place[1] ^ j))
                for j in range(1, n)
            ]
            + [pl.BlockSpec((EDGE, depth), lambda i, place, j=j: (last, place[1] ^ j)) for j in range(1, n)]
            + [pl.BlockSpec((dt_rows, depth), lambda i, place: (0, 0))],
            out_specs=[pl.BlockSpec((height, depth), lambda i, place: (0, 0))] * (n - 1),
        ),
        out_shape=[shape_of((height, depth), BF16)] * (n - 1),
        name="pack",
        compiler_params=params(58),
    )(place, *[tokens] * (2 * n - 2), dt_t)


def join_kernel(part, count, *refs):
    blocks, out = refs[:count], refs[-1]
    for i, block in enumerate(blocks):
        out[i * part : (i + 1) * part] = block[:part]


def join(blocks, part, after):
    depth = blocks[0].shape[1]
    return pl.pallas_call(
        functools.partial(join_kernel, part, len(blocks)),
        in_specs=[VMEM] * len(blocks) + [ANY] * len(after),
        out_specs=VMEM,
        out_shape=shape_of((part * len(blocks), depth), BF16),
        name="join",
        compiler_params=params(MAIN_MIB),
    )(*blocks, *after)


class Reduction:
    def __init__(self, blocks, order, weights):
        self.blocks, self.order, self.weights = blocks, order, weights
        self.part = blocks[0].shape[0]

    def rows(self, offsets, after):
        return chained([jnp.concatenate([self.blocks[j] for j in offsets], 0)], after)[0]

    def send(self, after):
        offsets = [j for j in range(len(self.blocks)) if j & self.order[0]]
        out = dot32(self.rows(offsets, after), self.weights).astype(BF16)
        self.got = swapped(out, "ctx", self.order[0])
        return out

    def keep(self, after):
        kept = [j for j in range(len(self.blocks)) if not j & self.order[0]]
        size = self.part
        got = [self.got[i * size : (i + 1) * size] for i in range(len(kept))]
        bit = self.order[1]
        gone = [i for i, j in enumerate(kept) if j & bit]
        stay = [i for i, j in enumerate(kept) if not j & bit]
        rows = self.rows([kept[i] for i in gone], after)
        out = (dot32(rows, self.weights) + jnp.concatenate([got[i] for i in gone], 0)).astype(BF16)
        mark = out
        arrived = swapped(out, "ctx", bit)
        rows = self.rows([kept[i] for i in stay], after)
        total = dot32(rows, self.weights) + jnp.concatenate([got[i] for i in stay], 0)
        kept = [kept[i] for i in stay]
        for bit in self.order[2:]:
            total = total + arrived.astype(F32)
            gone = [i for i, j in enumerate(kept) if j & bit]
            stay = [i for i, j in enumerate(kept) if not j & bit]
            parts = [total[i * size : (i + 1) * size] for i in range(len(kept))]
            out = jnp.concatenate([parts[i] for i in gone], 0).astype(BF16)
            total = jnp.concatenate([parts[i] for i in stay], 0)
            arrived = swapped(out, "ctx", bit)
            kept = [kept[i] for i in stay]
        self.total, self.last = total, arrived
        return mark


def finished(total, last, scale):
    return ((total + last.astype(F32)) * scale).astype(BF16)


def finish_kernel(count, *refs):
    totals, lasts, scale_ref, outs = refs[:count], refs[count : 2 * count], refs[2 * count], refs[-count:]
    for total, last, out in zip(totals, lasts, outs):
        out[...] = finished(total[...], last[...], scale_ref[...])


def finish(name, totals, lasts, scale, after):
    count = len(totals)
    return pl.pallas_call(
        functools.partial(finish_kernel, count),
        in_specs=[VMEM] * (2 * count + 1) + [ANY] * len(after),
        out_specs=[VMEM] * count,
        out_shape=[shape_of(t.shape, BF16) for t in totals],
        cost_estimate=cost(4 * count * totals[0].size, 8 * count * totals[0].size),
        name=name,
        compiler_params=params(MAIN_MIB),
    )(*totals, *lasts, scale, *after)


def quarter_values(values, totals, lasts, scale):
    early = [v[...] for v in values]
    return early + [finished(t[...], l[...], scale) for t, l in zip(totals, lasts)]


def step_kernel(n, me_ref, tok_ref, *refs):
    weights, heads_ref = refs[:n], refs[n]
    shift_t_ref, cum_ref, fade_ref, log_ref, acc = refs[-5:]
    j = pl.program_id(0)

    @pl.when(j == 0)
    def _():
        acc[...] = jnp.zeros_like(acc)

    for i in range(n):

        @pl.when(j == i)
        def _():
            acc[...] += lax.dot_general(
                weights[i][...], tok_ref[...], (((1,), (1,)), ((), ())), preferred_element_type=F32
            )

    @pl.when(j == pl.num_programs(0) - 1)
    def _():
        v = acc[: heads_ref.shape[0]] + heads_ref[:, 0:1]
        step = jnp.maximum(v, 0.0) + jnp.log1p(jnp.exp(-jnp.abs(v)))
        rate = -jnp.exp(heads_ref[:, 1:2]) * step
        rows = rate.shape[1]
        up_to = lax.broadcasted_iota(jnp.int32, (rows, rows), 0) <= lax.broadcasted_iota(
            jnp.int32, (rows, rows), 1
        )
        cum = jnp.dot(
            rate, up_to.astype(F32), precision=lax.Precision.HIGHEST, preferred_element_type=F32
        )
        last = cum[:, rows - 1 : rows]
        shift_t_ref[...] = cum - jnp.log(step)
        cum_ref[...] = cum.T
        fade_ref[...] = (jnp.exp(last - cum) * step).T
        log_ref[...] = jnp.broadcast_to(last.T, log_ref.shape)


def step_sizes(place, tokens, dt_t, payloads, heads, after):
    dt_rows, depth = dt_t.shape
    local_heads = heads.shape[0]
    n = len(payloads) + 1
    rows = tokens.shape[0]
    last = payloads[0].shape[0] // dt_rows - 1
    whole = lambda shape: pl.BlockSpec(shape, lambda j, place: (0, 0))
    return pl.pallas_call(
        functools.partial(step_kernel, n),
        grid_spec=pltpu.PrefetchScalarGridSpec(
            num_scalar_prefetch=1,
            grid=(n,),
            in_specs=[
                pl.BlockSpec((rows, depth), lambda j, place: (0, place[1] ^ j)),
                whole((dt_rows, depth)),
            ]
            + [pl.BlockSpec((dt_rows, depth), lambda j, place: (last, 0))] * (n - 1)
            + [whole((local_heads, 3))]
            + [ANY] * len(after),
            out_specs=[
                whole((local_heads, rows)),
                whole((rows, local_heads)),
                whole((rows, local_heads)),
                whole((8, local_heads)),
            ],
            scratch_shapes=[pltpu.VMEM((dt_rows, rows), F32)],
        ),
        out_shape=[
            shape_of((local_heads, rows), F32),
            shape_of((rows, local_heads), F32),
            shape_of((rows, local_heads), F32),
            shape_of((8, local_heads), F32),
        ],
        cost_estimate=cost(2 * n * rows * depth * LANES, 2 * n * rows * depth),
        name="steps",
        compiler_params=params(MAIN_MIB),
    )(place, tokens, dt_t, *payloads, heads, *after)


def write_logs(state_ref, parts):
    rows = lax.broadcasted_iota(jnp.int32, (LOG_ROWS, state_ref.shape[1]), 0)
    block = jnp.zeros((LOG_ROWS, state_ref.shape[1]), F32)
    for i, one in enumerate(parts):
        block = jnp.where(rows == i, one, block)
    state_ref[N:] = block.astype(BF16)


def read_logs(state_ref):
    block = state_ref[N:].astype(F32)
    return sum(block[i : i + 1] for i in range(LOG_PARTS))


def split_logs(logs):
    parts = []
    for _ in range(LOG_PARTS):
        parts.append(logs.astype(BF16).astype(F32))
        logs = logs - parts[-1]
    return parts


def head_spread(local_heads):
    channels = local_heads * P_SIZE
    hit = (
        lax.broadcasted_iota(jnp.int32, (local_heads, channels), 1) // P_SIZE
        == lax.broadcasted_iota(jnp.int32, (local_heads, channels), 0)
    )
    return hit.astype(F32).astype(BF16)


def spread_heads(values, hits):
    high = values.astype(BF16)
    low = (values - high.astype(F32)).astype(BF16)
    return dot32(high, hits) + dot32(low, hits)


def conv_kernel(place_ref, *refs):
    values, totals, lasts = refs[:EARLY], refs[EARLY:SLOTS], refs[SLOTS : 2 * SLOTS - EARLY]
    arrived_ref, before_ref, scale_ref, taps_ref, fade_ref, log_ref = refs[2 * SLOTS - EARLY : 2 * SLOTS - EARLY + 6]
    conv_ref, state_ref, vals = refs[-3:]
    part, width = totals[0].shape
    rows = part * SLOTS
    channels = width - 2 * N
    slot = place_ref[0]
    first = place_ref[1] == 0
    vals[:EDGE] = jnp.where(first, before_ref[...].astype(F32), arrived_ref[...].astype(F32))
    for k, value in enumerate(quarter_values(values, totals, lasts, scale_ref[...])):
        start = pl.multiple_of(EDGE + (slot ^ k) * part, EDGE)
        vals[pl.ds(start, part)] = value[:part].astype(F32)
    for c in range(0, width, 2 * LANES):
        cols = slice(c, c + 2 * LANES)
        for r in range(0, rows, part):
            summed = taps_ref[K : K + 1, cols]
            for tap in range(K):
                at = r + EDGE - (K - 1) + tap
                summed = summed + taps_ref[tap : tap + 1, cols] * vals[at : at + part, cols]
            conv_ref[r : r + part, cols] = silu(summed).astype(BF16)
    hits = head_spread(channels // P_SIZE)
    faded = spread_heads(fade_ref[...], hits) * conv_ref[:, :channels].astype(F32)
    state_ref[:N] = lax.dot_general(
        conv_ref[:, channels : channels + N],
        faded.astype(BF16),
        (((0,), (0,)), ((), ())),
        preferred_element_type=F32,
    ).astype(BF16)
    left, parts = log_ref[...], []
    for _ in range(LOG_PARTS):
        parts.append(left.astype(BF16))
        left = left - parts[-1].astype(F32)
    spread = [dot32(one, hits)[0:1] for one in parts]
    write_logs(state_ref, spread)


def conv_and_state(place, values, totals, lasts, arrived, before, scale, taps, fade, logs, after):
    part, width = totals[0].shape
    rows = part * SLOTS
    return pl.pallas_call(
        conv_kernel,
        in_specs=[SMEM] + [VMEM] * (2 * SLOTS - EARLY + 6) + [ANY] * len(after),
        out_specs=[VMEM, VMEM],
        out_shape=[shape_of((rows, width), BF16), shape_of((N + LOG_ROWS, width - 2 * N), BF16)],
        scratch_shapes=[pltpu.VMEM((rows + EDGE, width), F32)],
        cost_estimate=cost(30 * rows * width, 12 * rows * width, 2 * rows * width),
        name="conv",
        compiler_params=params(MAIN_MIB),
    )(place, *values, *totals, *lasts, arrived, before, scale, taps, fade, logs, *after)


def inner_kernel(conv_ref, cum_ref, shift_t_ref, skip_ref, *refs):
    y_ref, scores = refs[-2:]
    rows, width = conv_ref.shape
    channels = width - 2 * N
    size = LANES
    blocks = rows // size
    nt = (((1,), (1,)), ((), ()))
    scores[...] = lax.dot_general(
        conv_ref[:, channels + N :], conv_ref[:, channels : channels + N], nt, preferred_element_type=F32
    )
    lower = lax.broadcasted_iota(jnp.int32, (size, size), 0) >= lax.broadcasted_iota(
        jnp.int32, (size, size), 1
    )
    left = lax.broadcasted_iota(jnp.int32, (size, 2 * P_SIZE), 1) < P_SIZE
    for pair in range(channels // (2 * P_SIZE)):
        cols = slice(pair * 2 * P_SIZE, (pair + 1) * 2 * P_SIZE)
        for a in range(blocks):
            t = slice(a * size, (a + 1) * size)
            products = []
            for h in (2 * pair, 2 * pair + 1):
                here = cum_ref[t, h : h + 1]
                own = jnp.where(lower, here - shift_t_ref[h : h + 1, t], -jnp.inf)
                weights = jnp.exp(own) * scores[t, t]
                if a > 0:
                    before = slice(0, a * size)
                    earlier = jnp.exp(here - shift_t_ref[h : h + 1, before]) * scores[t, before]
                    weights = jnp.concatenate([earlier, weights], 1)
                products.append(dot32(weights.astype(BF16), conv_ref[: (a + 1) * size, cols]))
            y_ref[t, cols] = jnp.where(left, products[0], products[1]) + skip_ref[:, cols] * conv_ref[
                t, cols
            ].astype(F32)


def inner_output(conved, cum, shift_t, skip, after):
    rows, width = conved.shape
    channels = width - 2 * N
    return pl.pallas_call(
        inner_kernel,
        in_specs=[VMEM] * 4 + [ANY] * len(after),
        out_specs=VMEM,
        out_shape=shape_of((rows, channels), F32),
        scratch_shapes=[pltpu.VMEM((rows, rows), F32)],
        cost_estimate=cost(2 * rows * rows * channels, 8 * rows * width, rows * rows * channels // P_SIZE),
        name="inner",
        compiler_params=params(MAIN_MIB),
    )(conved, cum, shift_t, skip, *after)


def merge_kernel(index, place_ref, own_ref, got_ref, *refs):
    out_ref = refs[-1]
    own_log, got_log = read_logs(own_ref), read_logs(got_ref)
    own, got = own_ref[:N].astype(F32), got_ref[:N].astype(F32)
    later = place_ref[index] > 0
    own_fall = jnp.where(later, 1.0, jnp.exp(got_log))
    got_fall = jnp.where(later, jnp.exp(own_log), 1.0)
    out_ref[:N] = (own_fall * own + got_fall * got).astype(BF16)
    write_logs(out_ref, split_logs(own_log + got_log))


def merged(index, place, own, got, after):
    return pl.pallas_call(
        functools.partial(merge_kernel, index),
        in_specs=[SMEM, VMEM, VMEM] + [ANY] * len(after),
        out_specs=VMEM,
        out_shape=shape_of(own.shape, BF16),
        cost_estimate=cost(4 * own.size, 6 * own.size),
        name="merge",
        compiler_params=params(MAIN_MIB),
    )(place, own, got, *after)


def final_kernel(whole_group, rounds, place_ref, *refs):
    values, totals, lasts = refs[:EARLY], refs[EARLY:SLOTS], refs[SLOTS : 2 * SLOTS - EARLY]
    refs = refs[2 * SLOTS - EARLY :]
    gots, refs = refs[:rounds], refs[rounds:]
    y_ref, conv_ref, init_ref, cum_ref, scale_ref, gain_ref = refs[:6]
    outs = refs[6:]
    part, channels = totals[0].shape
    slot = place_ref[0]
    hits = head_spread(channels // P_SIZE)
    state = jnp.zeros((N, channels), F32)
    log = jnp.zeros((1, channels), F32)
    for i, got in enumerate(gots):
        later = place_ref[2 + i] > 0
        state = state + jnp.where(later, jnp.exp(log), 0.0) * got[:N].astype(F32)
        log = log + jnp.where(later, read_logs(got), 0.0)
    state = state.astype(BF16)
    init = init_ref[...].astype(BF16)
    init_fall = jnp.exp(log)
    nt = (((1,), (1,)), ((), ()))
    for k, value in enumerate(quarter_values(values, totals, lasts, scale_ref[...])):
        at = pl.ds(pl.multiple_of((slot ^ k) * part, part), part)
        c_part = conv_ref[at, channels + N :]
        carried = dot32(c_part, state)
        carried = carried + init_fall * lax.dot_general(c_part, init, nt, preferred_element_type=F32)
        y = y_ref[at] + carried * spread_heads(jnp.exp(cum_ref[at]), hits)
        gated = y * silu(value.astype(F32))
        squares = jnp.sum(gated * gated, axis=1, keepdims=True)
        if whole_group:
            meansq = squares / (H // G * P_SIZE)
            outs[0][at] = (gated * lax.rsqrt(meansq + 1e-05) * gain_ref[...]).astype(BF16)
        else:
            outs[0][at] = gated
            outs[1][at] = jnp.broadcast_to(squares, (part, LANES))


def final_output(whole_group, place, values, totals, lasts, gots, y, conved, init, cum, scale, gain):
    rows, channels = y.shape
    if whole_group:
        outs = [shape_of((rows, channels), BF16)]
    else:
        outs = [shape_of((rows, channels), F32), shape_of((rows, LANES), F32)]
    return pl.pallas_call(
        functools.partial(final_kernel, whole_group, len(gots)),
        in_specs=[SMEM] + [VMEM] * (2 * SLOTS - EARLY + 6 + len(gots)),
        out_specs=[VMEM] * len(outs),
        out_shape=outs,
        cost_estimate=cost(2 * rows * channels * N, 12 * rows * channels, 2 * rows * channels),
        name="final",
        compiler_params=params(MAIN_MIB),
    )(place, *values, *totals, *lasts, *gots, y, conved, init, cum, scale, gain)


def body(
    tokens,
    w_zx,
    zx_scale,
    w_bc,
    bc_scale,
    w_dt,
    conv_x,
    conv_bc,
    tail_x,
    tail_bc,
    head_params,
    init_state,
    norm_gain,
):
    tok_rows = tokens.shape[0]
    depth = w_zx.shape[0]
    local_heads = head_params.shape[1]
    channels = local_heads * P_SIZE
    per_group = H // G
    n_ctx = lax.axis_size("ctx")
    me = lax.axis_index("ctx")
    head_place = lax.axis_index("head")
    group_index = head_place * local_heads // per_group
    bits = [1 << i for i in range(n_ctx.bit_length() - 1)]
    part = tok_rows // SLOTS
    slot = head_place % SLOTS
    later = [((me & bit) > 0).astype(jnp.int32) for bit in bits]
    place = jnp.stack([slot.astype(jnp.int32), me.astype(jnp.int32)] + later)

    dt_t = w_dt.T
    if local_heads % EDGE:
        dt_t = jnp.pad(dt_t, ((0, EDGE - local_heads % EDGE), (0, 0)))
    payloads = pack(place, tokens, dt_t, n_ctx)
    payloads = [swapped(one, "ctx", j) for j, one in enumerate(payloads, 1)]
    w_all = jnp.transpose(w_zx, (1, 0, 2))
    bc_rows = pick_group(w_bc, group_index, 1)
    gate_w = w_all[0]
    first_w = jnp.concatenate([w_all[1], bc_rows], 1)
    fetched = join(payloads, part, (w_all, first_w))
    from_chip = swapped(fetched, "head", 2)
    from_core = swapped(fetched, "head", 1)


    own_rows = lax.dynamic_slice_in_dim(tokens, me * depth, depth, 1)

    def quarter(k, rows):
        order = bits if k in (0, 3) else bits[::-1]
        own = lax.dynamic_slice_in_dim(own_rows, (slot ^ k) * part, part, 0)
        first = gate = [own, *rows]
        if k == 0:
            gate = [own, *[one[:part] for one in rows]]
            first = [jnp.concatenate([own, own_rows[tok_rows - EDGE :]], 0), *rows]
        return Reduction(first, order, first_w), Reduction(gate, order, gate_w)

    def blocks_of(rows):
        return [rows[i * part : (i + 1) * part] for i in range(n_ctx - 1)]

    first0, gate0 = quarter(0, [one[: part + EDGE] for one in payloads])
    first1, gate1 = quarter(1, blocks_of(from_core))
    mark = first0.send(fetched)
    mark = first1.send(mark)
    mark = gate0.send(mark)
    mark = gate1.send(mark)
    shift_t, cum, fade, logs = step_sizes(place, tokens, dt_t, payloads, head_params.T, (mark,))
    mark = first0.keep(cum)
    mark = first1.keep(mark)
    mark = gate0.keep(mark)
    mark = gate1.keep(mark)
    scale = jnp.concatenate([zx_scale[1], pick_group(bc_scale, group_index, 0)], 0)[None]
    firsts01 = finish(
        "fin_first", (first0.total, first1.total), (first0.last, first1.last), scale, (mark,)
    )
    mark = firsts01[0]
    arrived = passed_along(firsts01[0][part:], "ctx", 1)
    from_both = swapped(chained([from_chip], mark)[0], "head", 1)
    first2, gate2 = quarter(2, blocks_of(from_chip))
    first3, gate3 = quarter(3, blocks_of(from_both))
    mark = first2.send(mark)
    mark = first3.send(mark)
    gates01 = finish("fin_gate", (gate0.total, gate1.total), (gate0.last, gate1.last), zx_scale[0:1], (mark,))
    mark = gates01[0]
    mark = first2.keep(mark)
    mark = first3.keep(mark)
    mark = gate2.send(mark)
    mark = gate3.send(mark)

    taps = jnp.concatenate([conv_x, pick_group(conv_bc, group_index, 1)], 1)
    before = jnp.concatenate([tail_x, pick_group(tail_bc, group_index, 1)], 1)
    before = jnp.pad(before, ((EDGE - (K - 1), 0), (0, 0)))
    conved, local_state = conv_and_state(
        place, firsts01, (first2.total, first3.total), (first2.last, first3.last), arrived, before, scale, taps, fade, logs, (mark,)
    )
    mark = gate2.keep(conved)
    mark = gate3.keep(mark)
    y_local = inner_output(conved, cum, shift_t, jnp.repeat(head_params[2], P_SIZE)[None], (mark,))

    run, gots = local_state, []
    for i, bit in enumerate(bits):
        if bit == bits[-1]:
            gots.append(passed_along(run, "ctx", bit))
        else:
            gots.append(swapped(run, "ctx", bit))
            run = merged(2 + i, place, run, gots[-1], (mark,))

    whole_group = local_heads >= per_group
    outs = final_output(
        whole_group,
        place,
        gates01,
        (gate2.total, gate3.total),
        (gate2.last, gate3.last),
        gots,
        y_local,
        conved,
        init_state.reshape(channels, N),
        cum,
        zx_scale[0:1],
        norm_gain[None],
    )
    if whole_group:
        return outs[0]
    gated, squares = outs
    slot_hits = (jnp.arange(G) == group_index).astype(F32)
    group_sums = lax.psum(slot_hits[:, None] * squares[:, 0][None, :], "head")
    totals = lax.dynamic_index_in_dim(group_sums, group_index, 0, keepdims=False)
    meansq = totals / (per_group * P_SIZE)
    return (gated * lax.rsqrt(meansq + 1e-05)[:, None] * norm_gain).astype(BF16)


def solution(mesh):
    return jax.shard_map(
        body,
        mesh=mesh,
        in_specs=(
            P("ctx", None),
            P("ctx", None, "head"),
            P(None, "head"),
            P("ctx", None, None),
            P(),
            P("ctx", "head"),
            P(None, "head"),
            P(),
            P(None, "head"),
            P(),
            P(None, "head"),
            P("head", None, None),
            P("head"),
        ),
        out_specs=P("ctx", "head"),
        check_vma=False,
    )
```

profile of v0, /device:TPU:0, one launch (start us, length us, event | category | flops | bytes accessed | tf_op | source)
XLA Modules:
  0.0 180.8 jit_solution(3684385097515610401)
XLA Ops:
  0.6 3.5 %pack.1 = (bf16[160,2048]{1,0:T(8,128)(2,1)}, bf16[160,2048]{1,0:T(8,128)(2,1)}, bf16[160,2048]{1,0:T(8,128)(2,1)}) custom-call(s32[4]{0:T(128)} %pad_add_fusion.place_ref.me_ref, bf16[512,8192]{1,0:T(8,128)(2,1)} %tok_ref.1, bf16[512,8192]{1,0:T(8,128)(2,1)} %tok_ref.1, bf16[512,8192]{1,0:T(8,128)(2,1)} %tok_ref.1, bf16[512,8192]{1,0:T(8,128)(2,1)} %tok_ref.1, ...), custom_call_target="tpu_custom_call" | custom-call | tf_op jit(solution)/shard_map/pack/pallas_call | solution.py:85
  4.1 3.9 %collective-permute-start.2 = (bf16[160,2048]{1,0:T(8,128)(2,1)}, bf16[160,2048]{1,0:T(8,128)(2,1)S(1)}, u32[]{:S(2)}, u32[]{:S(2)}) collective-permute-start(bf16[160,2048]{1,0:T(8,128)(2,1)} %get-tuple-element.45), channel_id=1, source_target_pairs={{0,24},{8,16},{16,8},{24,0},{1,25},{9,17},{17,9},{25,1},{2,26},{10... | collective-permute-start | bytes 1966088 | tf_op jit(solution)/shard_map/ppermute | solution.py:56
  8.7 9.4 %copy.27 = bf16[2048,2,1024]{2,0,1:T(8,128)(2,1)} copy(bf16[2048,2,1024]{2,1,0:T(2,128)(2,1)} %param.14) | data formatting | bytes 16777216 | tf_op args[1]
  18.1 8.4 %constant_dynamic-slice_fusion.3 = bf16[2048,1,512]{2,1,0:T(2,128)(2,1)S(1)} fusion(bf16[2048,8,512]{2,1,0:T(8,128)(2,1)} %param.16, s32[]{:T(128)S(6)} %select_n.52), kind=kLoop, calls=%fused_computation.52 | loop fusion | bytes 4194308 | tf_op jit(solution)/shard_map/jit(dynamic_index_in_dim)/dynamic_slice | solution.py:60
  26.5 1.9 %copy.28 = bf16[2048,1,512]{2,0,1:T(8,128)(2,1)} copy(bf16[2048,1,512]{2,1,0:T(2,128)(2,1)S(1)} %constant_dynamic-slice_fusion.3) | data formatting | bytes 4194304
  28.4 2.5 %slice_bitcast_fusion.1 = bf16[2048,1024]{1,0:T(8,128)(2,1)} fusion(bf16[2,2048,1024]{2,1,0:T(8,128)(2,1)S(1)} %bitcast.86), kind=kLoop, calls=%fused_computation.3 | loop fusion | bytes 8388608 | tf_op jit(solution)/shard_map/squeeze | solution.py:515
  32.6 3.7 %fusion.15 = (bf16[128,2048]{1,0:T(8,128)(2,1)S(1)}, bf16[128,2048]{1,0:T(8,128)(2,1)}, bf16[128,2048]{1,0:T(8,128)(2,1)S(1)}, bf16[128,2048]{1,0:T(8,128)(2,1)}) fusion(bf16[512,8192]{1,0:T(8,128)(2,1)} %tok_ref.1, s32[]{:T(128)S(6)} %select_n.58, s32[]{:T(128)S(6)} %select_n.50, s32[]{:T(128)S(6)} %select_n.54, s32[]{:T(128)S(6)} %select_n.48, s32[]{:T(128)S(6)} %select_n.56), kind=kLoop, calls=%fused_computation.59 | loop fusion | bytes 4194324 | tf_op jit(solution)/shard_map/dynamic_slice | solution.py:525
  36.3 3.4 %pad_maximum_fusion.refs_4_ = bf16[2048,1536]{1,0:T(8,128)(2,1)S(1)} fusion(bf16[2048,512]{1,0:T(8,128)(2,1)} %bitcast.107, bf16[2048,1024]{1,0:T(8,128)(2,1)} %slice_bitcast_fusion.1), kind=kLoop, calls=%fused_computation.1 | loop fusion | flops 12582912 | bytes 12582912 | tf_op jit(solution)/shard_map/concatenate | solution.py:515
  39.7 3.4 %copy-done.3 = bf16[2048,2,1024]{2,0,1:T(8,128)(2,1)S(1)} copy-done((bf16[2048,2,1024]{2,0,1:T(8,128)(2,1)S(1)}, bf16[2048,2,1024]{2,0,1:T(8,128)(2,1)}, u32[]{:S(2)}) %copy-start.3) | copy-done | bytes 8388632
  43.4 2.1 %collective-permute-start.10 = (bf16[384,2048]{1,0:T(8,128)(2,1)S(1)}, bf16[384,2048]{1,0:T(8,128)(2,1)S(1)}, u32[]{:S(2)}, u32[]{:S(2)}) collective-permute-start(bf16[384,2048]{1,0:T(8,128)(2,1)S(1)} %join.1), channel_id=1, source_target_pairs={{0,2},{1,3},{2,0},{3,1},{4,6},{5,7},{6,4},{7,5},{8,10},{9,11},{10,... | collective-permute-start | bytes 4718600 | tf_op jit(solution)/shard_map/ppermute | solution.py:56
  45.7 2.9 %convolution_convert_fusion = bf16[288,1536]{1,0:T(8,128)(2,1)} fusion(bf16[288,2048]{1,0:T(8,128)(2,1)S(1)} %pad_maximum_fusion.1, bf16[2048,1536]{1,0:T(8,128)(2,1)S(1)} %pad_maximum_fusion.refs_4_), kind=kOutput, calls=%fused_computation.4 | convolution fusion | flops 1812381696 | bytes 8355840 | tf_op jit(solution)/shard_map/dot_general | solution.py:64
  48.6 1.5 collective-permute-start.4
  51.6 2.7 %convolution_convert_fusion.3 = bf16[256,1536]{1,0:T(8,128)(2,1)} fusion(bf16[256,2048]{1,0:T(8,128)(2,1)S(1)} %concatenate.43, bf16[2048,1536]{1,0:T(8,128)(2,1)S(1)} %pad_maximum_fusion.refs_4_), kind=kOutput, calls=%fused_computation.7 | convolution fusion | flops 1611005952 | bytes 8126464 | tf_op jit(solution)/shard_map/dot_general | solution.py:64
  55.3 2.1 %convolution_convert_fusion.7 = bf16[256,1024]{1,0:T(8,128)(2,1)} fusion(bf16[256,2048]{1,0:T(8,128)(2,1)S(1)} %pad_maximum_fusion.2, bf16[2,2048,1024]{2,1,0:T(8,128)(2,1)S(1)} %bitcast.90), kind=kOutput, calls=%fused_computation.20 | convolution fusion | flops 1074003968 | bytes 5767168 | tf_op jit(solution)/shard_map/dot_general | solution.py:64
  57.9 1.5 collective-permute-start.5
  61.3 4.7 %steps.1 = (f32[16,512]{1,0:T(8,128)S(1)}, f32[512,16]{1,0:T(8,128)S(1)}, f32[512,16]{1,0:T(8,128)S(1)}, f32[8,16]{1,0:T(8,128)S(1)}) custom-call(s32[4]{0:T(128)S(1)} %copy-done.7, bf16[512,8192]{1,0:T(8,128)(2,1)S(1)} %bitcast.85, bf16[16,2048]{1,0:T(8,128)(2,1)S(1)} %bitcast.104, bf16[160,2048]{1,0:T(8,128)(2,1)S(1)} %collective-permute-done.refs_0_.refs_1_, ...), custom_call_target="tpu_custom_call" | custom-call | flops 16777216 | bytes 131072 | tf_op jit(solution)/shard_map/steps/pallas_call | solution.py:234
  66.0 5.4 %collective-permute-done.4 = bf16[288,1536]{1,0:T(8,128)(2,1)} collective-permute-done((bf16[288,1536]{1,0:T(8,128)(2,1)}, bf16[288,1536]{1,0:T(8,128)(2,1)}, u32[]{:S(2)}, u32[]{:S(2)}) %collective-permute-start.4) | collective-permute-done | bytes 884768 | tf_op jit(solution)/shard_map/ppermute | solution.py:56
  71.4 2.1 %fusion = bf16[144,1536]{1,0:T(8,128)(2,1)S(1)} fusion(bf16[144,2048]{1,0:T(8,128)(2,1)S(1)} %slice.148, bf16[2048,1536]{1,0:T(8,128)(2,1)S(1)} %pad_maximum_fusion.refs_4_, bf16[288,1536]{1,0:T(8,128)(2,1)} %collective-permute-done.4), kind=kOutput, calls=%fused_computation.12 | convolution fusion | flops 906633216 | bytes 7766016 | tf_op jit(solution)/shard_map/dot_general | solution.py:64
  73.6 1.6 collective-permute-start.11
  76.3 2.2 %convert_add_fusion.refs_0_ = f32[144,1536]{1,0:T(8,128)S(1)} fusion(bf16[288,1536]{1,0:T(8,128)(2,1)} %collective-permute-done.4, bf16[144,2048]{1,0:T(8,128)(2,1)S(1)} %pad_maximum_fusion.4, bf16[2048,1536]{1,0:T(8,128)(2,1)S(1)} %pad_maximum_fusion.refs_4_), kind=kOutput, calls=%fused_computation.32 | convolution fusion | flops 906412032 | bytes 8208384 | tf_op jit(solution)/shard_map/dot_general | solution.py:64
  78.7 2.0 %fusion.1 = bf16[128,1536]{1,0:T(8,128)(2,1)S(1)} fusion(bf16[128,2048]{1,0:T(8,128)(2,1)S(1)} %slice.147, bf16[2048,1536]{1,0:T(8,128)(2,1)S(1)} %pad_maximum_fusion.refs_4_, bf16[256,1536]{1,0:T(8,128)(2,1)} %collective-permute-done.5), kind=kOutput, calls=%fused_computation.13 | convolution fusion | flops 805896192 | bytes 7602176 | tf_op jit(solution)/shard_map/dot_general | solution.py:64
  80.8 1.6 collective-permute-start.12
  82.3 2.0 %convert_add_fusion.3.refs_1_ = f32[128,1536]{1,0:T(8,128)S(1)} fusion(bf16[256,1536]{1,0:T(8,128)(2,1)} %collective-permute-done.5, bf16[128,2048]{1,0:T(8,128)(2,1)S(1)} %copy-done.10, bf16[2048,1536]{1,0:T(8,128)(2,1)S(1)} %pad_maximum_fusion.refs_4_), kind=kOutput, calls=%fused_computation.35 | convolution fusion | flops 805699584 | bytes 7995392 | tf_op jit(solution)/shard_map/dot_general | solution.py:64
  84.4 1.7 fusion.4
  86.1 3.9 %collective-permute-done.7 = bf16[256,1024]{1,0:T(8,128)(2,1)} collective-permute-done((bf16[256,1024]{1,0:T(8,128)(2,1)S(1)}, bf16[256,1024]{1,0:T(8,128)(2,1)}, u32[]{:S(2)}, u32[]{:S(2)}) %collective-permute-start.7) | collective-permute-done | bytes 524320 | tf_op jit(solution)/shard_map/ppermute | solution.py:56
  89.9 1.7 fusion.5.refs_5_
  91.6 6.3 %collective-permute-done.11.refs_2_ = bf16[144,1536]{1,0:T(8,128)(2,1)S(1)} collective-permute-done((bf16[144,1536]{1,0:T(8,128)(2,1)S(1)}, bf16[144,1536]{1,0:T(8,128)(2,1)S(1)}, u32[]{:S(2)}, u32[]{:S(2)}) %collective-permute-start.11) | collective-permute-done | bytes 442400 | tf_op jit(solution)/shard_map/ppermute | solution.py:56
  98.4 1.6 collective-permute-start.8
  100.0 1.5 collective-permute-start.9
  101.5 1.7 convert_add_fusion.7.refs_0_
  103.1 1.7 convert_add_fusion.6.refs_1_
  104.8 1.8 %convolution_convert_fusion.2 = bf16[256,1536]{1,0:T(8,128)(2,1)S(1)} fusion(bf16[256,2048]{1,0:T(8,128)(2,1)S(1)} %concatenate.44, bf16[2048,1536]{1,0:T(8,128)(2,1)S(1)} %pad_maximum_fusion.refs_4_), kind=kOutput, calls=%fused_computation.6 | convolution fusion | flops 1611005952 | bytes 8126464 | tf_op jit(solution)/shard_map/dot_general | solution.py:64
  107.3 2.6 %collective-permute-start.18 = (bf16[16,1536]{1,0:T(8,128)(2,1)S(1)}, bf16[16,1536]{1,0:T(8,128)(2,1)S(1)}, u32[]{:S(2)}, u32[]{:S(2)}) collective-permute-start(bf16[16,1536]{1,0:T(8,128)(2,1)S(1)} %slice.140), channel_id=1, source_target_pairs={{0,8},{8,16},{16,24},{1,9},{9,17},{17,25},{2,10},{10,18},{18,26},{... | collective-permute-start | bytes 147464 | tf_op jit(solution)/shard_map/ppermute | solution.py:51
  110.2 1.8 %convolution_convert_fusion.1.refs_5_ = bf16[256,1536]{1,0:T(8,128)(2,1)S(1)} fusion(bf16[256,2048]{1,0:T(8,128)(2,1)S(1)} %pad_maximum_fusion.3, bf16[2048,1536]{1,0:T(8,128)(2,1)S(1)} %pad_maximum_fusion.refs_4_), kind=kOutput, calls=%fused_computation.5 | convolution fusion | flops 1611005952 | bytes 8126464 | tf_op jit(solution)/shard_map/dot_general | solution.py:64
  112.1 2.5 %collective-permute-start.15 = (bf16[256,1536]{1,0:T(8,128)(2,1)S(1)}, bf16[256,1536]{1,0:T(8,128)(2,1)S(1)}, u32[]{:S(2)}, u32[]{:S(2)}) collective-permute-start(bf16[256,1536]{1,0:T(8,128)(2,1)S(1)} %convolution_convert_fusion.1.refs_5_), channel_id=1, source_target_pairs={{0,8},{8,0},{16,24},{24,16},{1,9},{9,1},{17,25},{25,17},{2,10},{10... | collective-permute-start | bytes 2359304 | tf_op jit(solution)/shard_map/ppermute | solution.py:56
  114.7 11.4 %collective-permute-done.14 = bf16[256,1536]{1,0:T(8,128)(2,1)S(1)} collective-permute-done((bf16[256,1536]{1,0:T(8,128)(2,1)S(1)}, bf16[256,1536]{1,0:T(8,128)(2,1)S(1)}, u32[]{:S(2)}, u32[]{:S(2)}) %collective-permute-start.14) | collective-permute-done | bytes 786464 | tf_op jit(solution)/shard_map/ppermute | solution.py:56
  128.8 4.1 %collective-permute-done.15 = bf16[256,1536]{1,0:T(8,128)(2,1)S(1)} collective-permute-done((bf16[256,1536]{1,0:T(8,128)(2,1)S(1)}, bf16[256,1536]{1,0:T(8,128)(2,1)S(1)}, u32[]{:S(2)}, u32[]{:S(2)}) %collective-permute-start.15) | collective-permute-done | bytes 786464 | tf_op jit(solution)/shard_map/ppermute | solution.py:56
  135.2 1.3 convolution_convert_fusion.5
  138.7 2.1 %collective-permute-start.20 = (bf16[256,1024]{1,0:T(8,128)(2,1)S(1)}, bf16[256,1024]{1,0:T(8,128)(2,1)S(1)}, u32[]{:S(2)}, u32[]{:S(2)}) collective-permute-start(bf16[256,1024]{1,0:T(8,128)(2,1)S(1)} %convolution_convert_fusion.4.refs_12_), channel_id=1, source_target_pairs={{0,8},{8,0},{16,24},{24,16},{1,9},{9,1},{17,25},{25,17},{2,10},{10... | collective-permute-start | bytes 1572872 | tf_op jit(solution)/shard_map/ppermute | solution.py:56
  141.9 4.2 %collective-permute-done.17.refs_5_ = bf16[128,1536]{1,0:T(8,128)(2,1)S(1)} collective-permute-done((bf16[128,1536]{1,0:T(8,128)(2,1)S(1)}, bf16[128,1536]{1,0:T(8,128)(2,1)S(1)}, u32[]{:S(2)}, u32[]{:S(2)}) %collective-permute-start.17) | collective-permute-done | bytes 393248 | tf_op jit(solution)/shard_map/ppermute | solution.py:56
  146.1 4.9 %conv.1 = (bf16[512,1536]{1,0:T(8,128)(2,1)S(1)}, bf16[272,1024]{1,0:T(8,128)(2,1)S(1)}) custom-call(s32[4]{0:T(128)S(1)} %copy-done.7, bf16[144,1536]{1,0:T(8,128)(2,1)S(1)} %get-tuple-element.59.refs_0_, bf16[128,1536]{1,0:T(8,128)(2,1)S(1)} %get-tuple-element.65.refs_1_, f32[128,1536]{1,0:T(8,128)S(1)} %convert_add_fusion.2.refs_2_, ...), custom_call_target="tpu_custom_call" | custom-call | flops 368640 | bytes 147456 | tf_op jit(solution)/shard_map/conv/pallas_call | solution.py:342
  151.0 2.1 %collective-permute-start.23 = (bf16[272,1024]{1,0:T(8,128)(2,1)S(1)}, bf16[272,1024]{1,0:T(8,128)(2,1)S(1)}, u32[]{:S(2)}, u32[]{:S(2)}) collective-permute-start(bf16[272,1024]{1,0:T(8,128)(2,1)S(1)} %get-tuple-element.79.own_ref), channel_id=1, source_target_pairs={{0,8},{8,0},{16,24},{24,16},{1,9},{9,1},{17,25},{25,17},{2,10},{10... | collective-permute-start | bytes 1671176 | tf_op jit(solution)/shard_map/ppermute | solution.py:56
  154.7 1.5 collective-permute-start.21
  157.3 8.7 %collective-permute-done.23.got_ref.refs_6_ = bf16[272,1024]{1,0:T(8,128)(2,1)S(1)} collective-permute-done((bf16[272,1024]{1,0:T(8,128)(2,1)S(1)}, bf16[272,1024]{1,0:T(8,128)(2,1)S(1)}, u32[]{:S(2)}, u32[]{:S(2)}) %collective-permute-start.23) | collective-permute-done | bytes 557088 | tf_op jit(solution)/shard_map/ppermute | solution.py:56
  166.8 2.8 %collective-permute-start.24 = (bf16[272,1024]{1,0:T(8,128)(2,1)S(1)}, bf16[272,1024]{1,0:T(8,128)(2,1)S(1)}, u32[]{:S(2)}, u32[]{:S(2)}) collective-permute-start(bf16[272,1024]{1,0:T(8,128)(2,1)S(1)} %merge.1), channel_id=1, source_target_pairs={{0,16},{8,24},{1,17},{9,25},{2,18},{10,26},{3,19},{11,27},{4,20},{... | collective-permute-start | bytes 1671176 | tf_op jit(solution)/shard_map/ppermute | solution.py:51
  170.4 3.4 %inner.1.refs_8_ = f32[512,1024]{1,0:T(8,128)S(1)} custom-call(bf16[512,1536]{1,0:T(8,128)(2,1)S(1)} %get-tuple-element.74.conv_ref.refs_9_, f32[512,16]{1,0:T(8,128)S(1)} %get-tuple-element.50.cum_ref.refs_11_, f32[16,512]{1,0:T(8,128)S(1)} %get-tuple-element.80.shift_t_ref, f32[1,1024]{1,0:T(1,128)S(1)} %broadcast_in_dim_reshape.3.skip_ref, ...), custom_call_target="tpu_custom_call" | custom-call | flops 8388608 | bytes 98304 | tf_op jit(solution)/shard_map/inner/pallas_call | solution.py:390
  174.6 2.0 %collective-permute-done.24.refs_7_ = bf16[272,1024]{1,0:T(8,128)(2,1)S(1)} collective-permute-done((bf16[272,1024]{1,0:T(8,128)(2,1)S(1)}, bf16[272,1024]{1,0:T(8,128)(2,1)S(1)}, u32[]{:S(2)}, u32[]{:S(2)}) %collective-permute-start.24) | collective-permute-done | bytes 557088 | tf_op jit(solution)/shard_map/ppermute | solution.py:51
  176.6 3.9 %final.1 = bf16[512,1024]{1,0:T(8,128)(2,1)} custom-call(s32[4]{0:T(128)S(1)} %copy-done.7, bf16[128,1024]{1,0:T(8,128)(2,1)S(1)} %get-tuple-element.63.refs_0_, bf16[128,1024]{1,0:T(8,128)(2,1)S(1)} %get-tuple-element.64.refs_1_, f32[128,1024]{1,0:T(8,128)S(1)} %convert_add_fusion.5.refs_2_, f32[128,1024]{1,0:T(8,128)S(1)} %convert_add_fusion.4.refs_3_, ...), custom_call_target="tpu_custom_call" | custom-call | flops 4194304 | bytes 98304 | tf_op jit(solution)/shard_map/final/pallas_call | solution.py:466
  (117 shorter events, 24.1 us)
Async XLA Ops:
  0.0 32.4 %copy-start = (f32[5,8,512]{2,1,0:T(8,128)S(1)}, f32[5,8,512]{2,1,0:T(8,128)}, u32[]{:S(2)}) copy-start(f32[5,8,512]{2,1,0:T(8,128)} %param.20) | copy-start | bytes 245764
  0.6 8.0 %copy-start.15 = (f32[3,16]{1,0:T(4,128)S(1)}, f32[3,16]{1,0:T(4,128)}, u32[]{:S(2)}) copy-start(f32[3,16]{1,0:T(4,128)} %param.23) | copy-start | bytes 580
  4.1 35.5 %collective-permute-start.2 = (bf16[160,2048]{1,0:T(8,128)(2,1)}, bf16[160,2048]{1,0:T(8,128)(2,1)S(1)}, u32[]{:S(2)}, u32[]{:S(2)}) collective-permute-start(bf16[160,2048]{1,0:T(8,128)(2,1)} %get-tuple-element.45), channel_id=1, source_target_pairs={{0,24},{8,16},{16,8},{24,0},{1,25},{9,17},{17,9},{25,1},{2,26},{10... | collective-permute-start | bytes 1966088 | tf_op jit(solution)/shard_map/ppermute | solution.py:56
  8.0 31.7 %collective-permute-start = (bf16[160,2048]{1,0:T(8,128)(2,1)}, bf16[160,2048]{1,0:T(8,128)(2,1)S(1)}, u32[]{:S(2)}, u32[]{:S(2)}) collective-permute-start(bf16[160,2048]{1,0:T(8,128)(2,1)} %get-tuple-element.43), channel_id=1, source_target_pairs={{0,8},{8,0},{16,24},{24,16},{1,9},{9,1},{17,25},{25,17},{2,10},{10... | collective-permute-start | bytes 1966088 | tf_op jit(solution)/shard_map/ppermute | solution.py:56
  8.6 31.1 %collective-permute-start.1 = (bf16[160,2048]{1,0:T(8,128)(2,1)}, bf16[160,2048]{1,0:T(8,128)(2,1)S(1)}, u32[]{:S(2)}, u32[]{:S(2)}) collective-permute-start(bf16[160,2048]{1,0:T(8,128)(2,1)} %get-tuple-element.44), channel_id=1, source_target_pairs={{0,16},{8,24},{16,0},{24,8},{1,17},{9,25},{17,1},{25,9},{2,18},{10... | collective-permute-start | bytes 1966088 | tf_op jit(solution)/shard_map/ppermute | solution.py:56
  18.0 10.3 %copy-start.2 = (bf16[2048,2,1024]{2,0,1:T(8,128)(2,1)S(1)}, bf16[2048,2,1024]{2,0,1:T(8,128)(2,1)}, u32[]{:S(2)}) copy-start(bf16[2048,2,1024]{2,0,1:T(8,128)(2,1)} %copy.27) | copy-start | bytes 25165828
  26.4 4.4 %copy-start.14 = (f32[2,1024]{1,0:T(2,128)S(1)}, f32[2,1024]{1,0:T(2,128)}, u32[]{:S(2)}) copy-start(f32[2,1024]{1,0:T(2,128)} %param.15) | copy-start | bytes 24580
  36.3 7.0 %copy-start.13 = (bf16[3,1024]{1,0:T(4,128)(2,1)S(1)}, bf16[3,1024]{1,0:T(4,128)(2,1)}, u32[]{:S(2)}) copy-start(bf16[3,1024]{1,0:T(4,128)(2,1)} %param.21) | copy-start | bytes 18436
  39.7 3.7 %dynamic-slice-start = ((bf16[512,8192]{1,0:T(8,128)(2,1)}, s32[]{:T(128)}, s32[]{:T(128)}), bf16[16,2048]{1,0:T(8,128)(2,1)S(1)}, s32[]{:S(2)}) async-start(bf16[512,8192]{1,0:T(8,128)(2,1)} %tok_ref.1, s32[]{:T(128)} %add.114, s32[]{:T(128)} %select_n.49), calls=%async_computation.2 | async-start | bytes 131584 | tf_op jit(solution)/shard_map/slice | solution.py:529
  39.7 3.4 %copy-start.3 = (bf16[2048,2,1024]{2,0,1:T(8,128)(2,1)S(1)}, bf16[2048,2,1024]{2,0,1:T(8,128)(2,1)}, u32[]{:S(2)}) copy-start(bf16[2048,2,1024]{2,0,1:T(8,128)(2,1)} %copy.27) | copy-start | bytes 25165828
  43.1 18.2 %copy-start.4 = (bf16[160,2048]{1,0:T(8,128)(2,1)}, bf16[160,2048]{1,0:T(8,128)(2,1)S(1)}, u32[]{:S(2)}) copy-start(bf16[160,2048]{1,0:T(8,128)(2,1)S(1)} %collective-permute-done.1.refs_1_.refs_2_) | copy-start | bytes 1966084
  43.2 7.2 %collective-permute-start.3 = (bf16[384,2048]{1,0:T(8,128)(2,1)S(1)}, bf16[384,2048]{1,0:T(8,128)(2,1)S(1)}, u32[]{:S(2)}, u32[]{:S(2)}) collective-permute-start(bf16[384,2048]{1,0:T(8,128)(2,1)S(1)} %join.1), channel_id=1, source_target_pairs={{0,1},{1,0},{2,3},{3,2},{4,5},{5,4},{6,7},{7,6},{8,9},{9,8},{10,11... | collective-permute-start | bytes 4718600 | tf_op jit(solution)/shard_map/ppermute | solution.py:56
  43.4 54.8 %collective-permute-start.10 = (bf16[384,2048]{1,0:T(8,128)(2,1)S(1)}, bf16[384,2048]{1,0:T(8,128)(2,1)S(1)}, u32[]{:S(2)}, u32[]{:S(2)}) collective-permute-start(bf16[384,2048]{1,0:T(8,128)(2,1)S(1)} %join.1), channel_id=1, source_target_pairs={{0,2},{1,3},{2,0},{3,1},{4,6},{5,7},{6,4},{7,5},{8,10},{9,11},{10,... | collective-permute-start | bytes 4718600 | tf_op jit(solution)/shard_map/ppermute | solution.py:56
  48.6 22.8 %collective-permute-start.4 = (bf16[288,1536]{1,0:T(8,128)(2,1)}, bf16[288,1536]{1,0:T(8,128)(2,1)}, u32[]{:S(2)}, u32[]{:S(2)}) collective-permute-start(bf16[288,1536]{1,0:T(8,128)(2,1)} %convolution_convert_fusion), channel_id=1, source_target_pairs={{0,8},{8,0},{16,24},{24,16},{1,9},{9,1},{17,25},{25,17},{2,10},{10... | collective-permute-start | bytes 2654216 | tf_op jit(solution)/shard_map/ppermute | solution.py:56
  50.4 1.2 copy-start.11
  51.6 2.8 %slice-start.2 = ((s8[8388608]{0:T(1024)(128)(4,1)}), s8[4194304]{0:T(1024)(128)(4,1)S(1)}, s32[]{:S(2)}) async-start(s8[8388608]{0:T(1024)(128)(4,1)} %bitcast.88), calls=%async_computation.3 | async-start | bytes 8388608
  51.6 3.7 %slice-start.3 = ((s8[8388608]{0:T(1024)(128)(4,1)}), s8[4194304]{0:T(1024)(128)(4,1)S(1)}, s32[]{:S(2)}) async-start(s8[8388608]{0:T(1024)(128)(4,1)} %bitcast.88), calls=%async_computation.4 | async-start | bytes 8388608
  55.3 6.0 %slice-start = ((s8[8388608]{0:T(1024)(128)(4,1)}), s8[4194304]{0:T(1024)(128)(4,1)S(1)}, s32[]{:S(2)}) async-start(s8[8388608]{0:T(1024)(128)(4,1)} %bitcast.84), calls=%async_computation | async-start | bytes 8388608
  57.4 3.9 %slice-start.1 = ((s8[8388608]{0:T(1024)(128)(4,1)}), s8[4194304]{0:T(1024)(128)(4,1)S(1)}, s32[]{:S(2)}) async-start(s8[8388608]{0:T(1024)(128)(4,1)} %bitcast.84), calls=%async_computation.1 | async-start | bytes 8388608
  57.4 3.9 %copy-start.6 = (bf16[2048,16]{0,1:T(8,128)(2,1)S(1)}, bf16[2048,16]{0,1:T(8,128)(2,1)}, u32[]{:S(2)}) copy-start(bf16[2048,16]{0,1:T(8,128)(2,1)} %param.18) | copy-start | bytes 196612
  57.4 3.9 %copy-start.7 = (s32[4]{0:T(128)S(1)}, s32[4]{0:T(128)}, u32[]{:S(2)}) copy-start(s32[4]{0:T(128)} %pad_add_fusion.place_ref.me_ref) | copy-start | bytes 52
  57.4 27.0 %collective-permute-start.6 = (bf16[256,1024]{1,0:T(8,128)(2,1)}, bf16[256,1024]{1,0:T(8,128)(2,1)}, u32[]{:S(2)}, u32[]{:S(2)}) collective-permute-start(bf16[256,1024]{1,0:T(8,128)(2,1)} %convolution_convert_fusion.7), channel_id=1, source_target_pairs={{0,8},{8,0},{16,24},{24,16},{1,9},{9,1},{17,25},{25,17},{2,10},{10... | collective-permute-start | bytes 1572872 | tf_op jit(solution)/shard_map/ppermute | solution.py:56
  57.9 20.8 %collective-permute-start.5 = (bf16[256,1536]{1,0:T(8,128)(2,1)}, bf16[256,1536]{1,0:T(8,128)(2,1)}, u32[]{:S(2)}, u32[]{:S(2)}) collective-permute-start(bf16[256,1536]{1,0:T(8,128)(2,1)} %convolution_convert_fusion.3), channel_id=1, source_target_pairs={{0,16},{8,24},{16,0},{24,8},{1,17},{9,25},{17,1},{25,9},{2,18},{10... | collective-permute-start | bytes 2359304 | tf_op jit(solution)/shard_map/ppermute | solution.py:56
  60.7 29.2 %collective-permute-start.7 = (bf16[256,1024]{1,0:T(8,128)(2,1)S(1)}, bf16[256,1024]{1,0:T(8,128)(2,1)}, u32[]{:S(2)}, u32[]{:S(2)}) collective-permute-start(bf16[256,1024]{1,0:T(8,128)(2,1)S(1)} %convolution_convert_fusion.6.refs_5_), channel_id=1, source_target_pairs={{0,16},{8,24},{16,0},{24,8},{1,17},{9,25},{17,1},{25,9},{2,18},{10... | collective-permute-start | bytes 1572872 | tf_op jit(solution)/shard_map/ppermute | solution.py:56
  73.6 24.3 %collective-permute-start.11 = (bf16[144,1536]{1,0:T(8,128)(2,1)S(1)}, bf16[144,1536]{1,0:T(8,128)(2,1)S(1)}, u32[]{:S(2)}, u32[]{:S(2)}) collective-permute-start(bf16[144,1536]{1,0:T(8,128)(2,1)S(1)} %fusion), channel_id=1, source_target_pairs={{0,16},{8,24},{16,0},{24,8},{1,17},{9,25},{17,1},{25,9},{2,18},{10... | collective-permute-start | bytes 1327112 | tf_op jit(solution)/shard_map/ppermute | solution.py:56
  78.4 3.9 %copy-start.10 = (bf16[128,2048]{1,0:T(8,128)(2,1)S(1)}, bf16[128,2048]{1,0:T(8,128)(2,1)}, u32[]{:S(2)}) copy-start(bf16[128,2048]{1,0:T(8,128)(2,1)} %get-tuple-element.58) | copy-start | bytes 1572868
  78.4 5.9 %slice-start.4 = ((bf16[160,2048]{1,0:T(8,128)(2,1)}), bf16[128,2048]{1,0:T(8,128)(2,1)S(1)}, s32[]{:S(2)}) async-start(bf16[160,2048]{1,0:T(8,128)(2,1)} %copy-done.4), calls=%async_computation.5 | async-start | bytes 1048576 | tf_op jit(solution)/shard_map/slice | solution.py:528
  80.8 17.2 %collective-permute-start.12 = (bf16[128,1536]{1,0:T(8,128)(2,1)S(1)}, bf16[128,1536]{1,0:T(8,128)(2,1)S(1)}, u32[]{:S(2)}, u32[]{:S(2)}) collective-permute-start(bf16[128,1536]{1,0:T(8,128)(2,1)S(1)} %fusion.1), channel_id=1, source_target_pairs={{0,8},{8,0},{16,24},{24,16},{1,9},{9,1},{17,25},{25,17},{2,10},{10... | collective-permute-start | bytes 1179656 | tf_op jit(solution)/shard_map/ppermute | solution.py:56
  86.1 12.2 %copy-start.12 = (f32[5,1024]{1,0:T(8,128)S(1)}, f32[5,1024]{1,0:T(8,128)}, u32[]{:S(2)}) copy-start(f32[5,1024]{1,0:T(8,128)} %param.19) | copy-start | bytes 61444
  98.2 11.8 %collective-permute-start.13 = (bf16[384,2048]{1,0:T(8,128)(2,1)S(1)}, bf16[384,2048]{1,0:T(8,128)(2,1)S(1)}, u32[]{:S(2)}, u32[]{:S(2)}) collective-permute-start(bf16[384,2048]{1,0:T(8,128)(2,1)S(1)} %collective-permute-done.10), channel_id=1, source_target_pairs={{0,1},{1,0},{2,3},{3,2},{4,5},{5,4},{6,7},{7,6},{8,9},{9,8},{10,11... | collective-permute-start | bytes 4718600 | tf_op jit(solution)/shard_map/ppermute | solution.py:56
  98.4 16.1 %collective-permute-start.8 = (bf16[128,1024]{1,0:T(8,128)(2,1)S(1)}, bf16[128,1024]{1,0:T(8,128)(2,1)S(1)}, u32[]{:S(2)}, u32[]{:S(2)}) collective-permute-start(bf16[128,1024]{1,0:T(8,128)(2,1)S(1)} %fusion.4), channel_id=1, source_target_pairs={{0,16},{8,24},{16,0},{24,8},{1,17},{9,25},{17,1},{25,9},{2,18},{10... | collective-permute-start | bytes 786440 | tf_op jit(solution)/shard_map/ppermute | solution.py:56
  100.0 14.5 %collective-permute-start.9 = (bf16[128,1024]{1,0:T(8,128)(2,1)S(1)}, bf16[128,1024]{1,0:T(8,128)(2,1)S(1)}, u32[]{:S(2)}, u32[]{:S(2)}) collective-permute-start(bf16[128,1024]{1,0:T(8,128)(2,1)S(1)} %fusion.5.refs_5_), channel_id=1, source_target_pairs={{0,8},{8,0},{16,24},{24,16},{1,9},{9,1},{17,25},{25,17},{2,10},{10... | collective-permute-start | bytes 786440 | tf_op jit(solution)/shard_map/ppermute | solution.py:56
  106.7 19.4 %collective-permute-start.14 = (bf16[256,1536]{1,0:T(8,128)(2,1)S(1)}, bf16[256,1536]{1,0:T(8,128)(2,1)S(1)}, u32[]{:S(2)}, u32[]{:S(2)}) collective-permute-start(bf16[256,1536]{1,0:T(8,128)(2,1)S(1)} %convolution_convert_fusion.2), channel_id=1, source_target_pairs={{0,16},{8,24},{16,0},{24,8},{1,17},{9,25},{17,1},{25,9},{2,18},{10... | collective-permute-start | bytes 2359304 | tf_op jit(solution)/shard_map/ppermute | solution.py:56
  107.3 34.6 %collective-permute-start.18 = (bf16[16,1536]{1,0:T(8,128)(2,1)S(1)}, bf16[16,1536]{1,0:T(8,128)(2,1)S(1)}, u32[]{:S(2)}, u32[]{:S(2)}) collective-permute-start(bf16[16,1536]{1,0:T(8,128)(2,1)S(1)} %slice.140), channel_id=1, source_target_pairs={{0,8},{8,16},{16,24},{1,9},{9,17},{17,25},{2,10},{10,18},{18,26},{... | collective-permute-start | bytes 147464 | tf_op jit(solution)/shard_map/ppermute | solution.py:51
  112.1 15.7 %copy-start.9 = (bf16[128,2048]{1,0:T(8,128)(2,1)S(1)}, bf16[128,2048]{1,0:T(8,128)(2,1)}, u32[]{:S(2)}) copy-start(bf16[128,2048]{1,0:T(8,128)(2,1)} %get-tuple-element.75) | copy-start | bytes 1572868
  112.1 20.9 %collective-permute-start.15 = (bf16[256,1536]{1,0:T(8,128)(2,1)S(1)}, bf16[256,1536]{1,0:T(8,128)(2,1)S(1)}, u32[]{:S(2)}, u32[]{:S(2)}) collective-permute-start(bf16[256,1536]{1,0:T(8,128)(2,1)S(1)} %convolution_convert_fusion.1.refs_5_), channel_id=1, source_target_pairs={{0,8},{8,0},{16,24},{24,16},{1,9},{9,1},{17,25},{25,17},{2,10},{10... | collective-permute-start | bytes 2359304 | tf_op jit(solution)/shard_map/ppermute | solution.py:56
  127.1 14.7 %collective-permute-start.16 = (bf16[128,1536]{1,0:T(8,128)(2,1)S(1)}, bf16[128,1536]{1,0:T(8,128)(2,1)S(1)}, u32[]{:S(2)}, u32[]{:S(2)}) collective-permute-start(bf16[128,1536]{1,0:T(8,128)(2,1)S(1)} %fusion.2), channel_id=1, source_target_pairs={{0,8},{8,0},{16,24},{24,16},{1,9},{9,1},{17,25},{25,17},{2,10},{10... | collective-permute-start | bytes 1179656 | tf_op jit(solution)/shard_map/ppermute | solution.py:56
  134.0 12.1 %collective-permute-start.17 = (bf16[128,1536]{1,0:T(8,128)(2,1)S(1)}, bf16[128,1536]{1,0:T(8,128)(2,1)S(1)}, u32[]{:S(2)}, u32[]{:S(2)}) collective-permute-start(bf16[128,1536]{1,0:T(8,128)(2,1)S(1)} %fusion.3), channel_id=1, source_target_pairs={{0,16},{8,24},{16,0},{24,8},{1,17},{9,25},{17,1},{25,9},{2,18},{10... | collective-permute-start | bytes 1179656 | tf_op jit(solution)/shard_map/ppermute | solution.py:56
  136.5 17.2 %collective-permute-start.19 = (bf16[256,1024]{1,0:T(8,128)(2,1)S(1)}, bf16[256,1024]{1,0:T(8,128)(2,1)S(1)}, u32[]{:S(2)}, u32[]{:S(2)}) collective-permute-start(bf16[256,1024]{1,0:T(8,128)(2,1)S(1)} %convolution_convert_fusion.5), channel_id=1, source_target_pairs={{0,16},{8,24},{16,0},{24,8},{1,17},{9,25},{17,1},{25,9},{2,18},{10... | collective-permute-start | bytes 1572872 | tf_op jit(solution)/shard_map/ppermute | solution.py:56
  138.7 17.5 %collective-permute-start.20 = (bf16[256,1024]{1,0:T(8,128)(2,1)S(1)}, bf16[256,1024]{1,0:T(8,128)(2,1)S(1)}, u32[]{:S(2)}, u32[]{:S(2)}) collective-permute-start(bf16[256,1024]{1,0:T(8,128)(2,1)S(1)} %convolution_convert_fusion.4.refs_12_), channel_id=1, source_target_pairs={{0,8},{8,0},{16,24},{24,16},{1,9},{9,1},{17,25},{25,17},{2,10},{10... | collective-permute-start | bytes 1572872 | tf_op jit(solution)/shard_map/ppermute | solution.py:56
  151.0 15.0 %collective-permute-start.23 = (bf16[272,1024]{1,0:T(8,128)(2,1)S(1)}, bf16[272,1024]{1,0:T(8,128)(2,1)S(1)}, u32[]{:S(2)}, u32[]{:S(2)}) collective-permute-start(bf16[272,1024]{1,0:T(8,128)(2,1)S(1)} %get-tuple-element.79.own_ref), channel_id=1, source_target_pairs={{0,8},{8,0},{16,24},{24,16},{1,9},{9,1},{17,25},{25,17},{2,10},{10... | collective-permute-start | bytes 1671176 | tf_op jit(solution)/shard_map/ppermute | solution.py:56
  154.7 19.8 %collective-permute-start.21 = (bf16[128,1024]{1,0:T(8,128)(2,1)S(1)}, bf16[128,1024]{1,0:T(8,128)(2,1)S(1)}, u32[]{:S(2)}, u32[]{:S(2)}) collective-permute-start(bf16[128,1024]{1,0:T(8,128)(2,1)S(1)} %fusion.6), channel_id=1, source_target_pairs={{0,8},{8,0},{16,24},{24,16},{1,9},{9,1},{17,25},{25,17},{2,10},{10... | collective-permute-start | bytes 786440 | tf_op jit(solution)/shard_map/ppermute | solution.py:56
  156.9 17.6 %collective-permute-start.22 = (bf16[128,1024]{1,0:T(8,128)(2,1)S(1)}, bf16[128,1024]{1,0:T(8,128)(2,1)S(1)}, u32[]{:S(2)}, u32[]{:S(2)}) collective-permute-start(bf16[128,1024]{1,0:T(8,128)(2,1)S(1)} %fusion.7.refs_0_), channel_id=1, source_target_pairs={{0,16},{8,24},{16,0},{24,8},{1,17},{9,25},{17,1},{25,9},{2,18},{10... | collective-permute-start | bytes 786440 | tf_op jit(solution)/shard_map/ppermute | solution.py:56
  166.8 9.8 %collective-permute-start.24 = (bf16[272,1024]{1,0:T(8,128)(2,1)S(1)}, bf16[272,1024]{1,0:T(8,128)(2,1)S(1)}, u32[]{:S(2)}, u32[]{:S(2)}) collective-permute-start(bf16[272,1024]{1,0:T(8,128)(2,1)S(1)} %merge.1), channel_id=1, source_target_pairs={{0,16},{8,24},{1,17},{9,25},{2,18},{10,26},{3,19},{11,27},{4,20},{... | collective-permute-start | bytes 1671176 | tf_op jit(solution)/shard_map/ppermute | solution.py:51
  170.3 6.3 %copy-start.5 = (f32[16,64,256]{2,1,0:T(8,128)S(1)}, f32[16,64,256]{2,1,0:T(8,128)}, u32[]{:S(2)}) copy-start(f32[16,64,256]{2,1,0:T(8,128)} %param.24) | copy-start | bytes 3145732
  170.3 6.2 %copy-start.8 = (f32[1024]{0:T(1024)S(1)}, f32[1024]{0:T(1024)}, u32[]{:S(2)}) copy-start(f32[1024]{0:T(1024)} %param.25) | copy-start | bytes 12292
  170.4 10.2 %copy-start.1 = (f32[5,8,512]{2,1,0:T(8,128)S(1)}, f32[5,8,512]{2,1,0:T(8,128)}, u32[]{:S(2)}) copy-start(f32[5,8,512]{2,1,0:T(8,128)} %param.20) | copy-start | bytes 245764
where the time goes:
time: 184 us; the launch traced here: 181 us
  waiting for transfers between devices  47 us (26%)
  matrix products  37.5 us (20%)
  local copies, waits for them, and re-layouts  34.9 us (19%)
  starting transfers between devices  34.4 us (19%)
  Pallas kernels  21.7 us (12%)
  other arithmetic  4.38 us (2%)
    ppermute x23, waiting for transfers between devices, swapped(): return lax.ppermute(x, axis, [(i, i ^ by) for i in range(length)])  45 us
    dot_general x24, matrix products, dot32(): return jnp.dot(a, b, preferred_element_type=F32)  37.5 us
    ppermute x23, starting transfers between devices, swapped(): return lax.ppermute(x, axis, [(i, i ^ by) for i in range(length)])  29 us
    unnamed x45, local copies, waits for them, and re-layouts  16.9 us
    dynamic_slice x4, local copies, waits for them, and re-layouts, pick_group(): lax.dynamic_index_in_dim(values, group_index, axis_index, keepdims=False)  9.88 us
    ppermute x2, starting transfers between devices, passed_along(): return lax.ppermute(x, axis, pairs)  5.44 us
    pallas_call x1, Pallas kernels, conv_and_state(): pl.pallas_call(conv_kernel, in_specs=[SMEM] + [VMEM] * (2 * SLOTS - EARLY...  4.89 us
    pallas_call x1, Pallas kernels, step_sizes(): pl.pallas_call(functools.partial(step_kernel, n), grid_spec=pltpu.Prefetc...  4.71 us
  transfers between devices with their start and end apart: 25, of which 10 were waited for; matrix products, arithmetic and copies ran while one was open for 39% of the time, Pallas kernels for 8%

commit v1 on v0

--- a/solution.py
+++ b/solution.py
@@ -123,18 +123,20 @@
     def __init__(self, blocks, order, weights):
         self.blocks, self.order, self.weights = blocks, order, weights
         self.part = blocks[0].shape[0]
+        self.n = len(blocks) + 1
 
     def rows(self, offsets, after):
-        return chained([jnp.concatenate([self.blocks[j] for j in offsets], 0)], after)[0]
+        return chained([jnp.concatenate([self.blocks[j - 1] for j in offsets], 0)], after)[0]
 
     def send(self, after):
-        offsets = [j for j in range(len(self.blocks)) if j & self.order[0]]
+        offsets = [j for j in range(self.n) if j & self.order[0]]
         out = dot32(self.rows(offsets, after), self.weights).astype(BF16)
         self.got = swapped(out, "ctx", self.order[0])
         return out
 
-    def keep(self, after):
-        kept = [j for j in range(len(self.blocks)) if not j & self.order[0]]
+    def keep(self, own, after):
+        self.blocks = [*self.blocks, own]
+        kept = [j for j in range(self.n) if not j & self.order[0]]
         size = self.part
         got = [self.got[i * size : (i + 1) * size] for i in range(len(kept))]
         bit = self.order[1]
@@ -512,52 +514,44 @@
     w_all = jnp.transpose(w_zx, (1, 0, 2))
     bc_rows = pick_group(w_bc, group_index, 1)
     gate_w = w_all[0]
-    first_w = jnp.concatenate([w_all[1], bc_rows], 1)
-    fetched = join(payloads, part, (w_all, first_w))
+    fetched = join(payloads, part, (gate_w, bc_rows))
     from_chip = swapped(fetched, "head", 2)
     from_core = swapped(fetched, "head", 1)
 
-
-    own_rows = lax.dynamic_slice_in_dim(tokens, me * depth, depth, 1)
-
-    def quarter(k, rows):
-        order = bits if k in (0, 3) else bits[::-1]
-        own = lax.dynamic_slice_in_dim(own_rows, (slot ^ k) * part, part, 0)
-        first = gate = [own, *rows]
-        if k == 0:
-            gate = [own, *[one[:part] for one in rows]]
-            first = [jnp.concatenate([own, own_rows[tok_rows - EDGE :]], 0), *rows]
-        return Reduction(first, order, first_w), Reduction(gate, order, gate_w)
-
     def blocks_of(rows):
         return [rows[i * part : (i + 1) * part] for i in range(n_ctx - 1)]
 
-    first0, gate0 = quarter(0, [one[: part + EDGE] for one in payloads])
-    first1, gate1 = quarter(1, blocks_of(from_core))
-    mark = first0.send(fetched)
+    gate0 = Reduction([one[:part] for one in payloads], bits, gate_w)
+    gate1 = Reduction(blocks_of(from_core), bits[::-1], gate_w)
+    mark = gate0.send(fetched)
+    mark = gate1.send(mark)
+    first_w = jnp.concatenate([w_all[1], chained([bc_rows], mark)[0]], 1)
+    first0 = Reduction([one[: part + EDGE] for one in payloads], bits, first_w)
+    first1 = Reduction(blocks_of(from_core), bits[::-1], first_w)
+    mark = first0.send(mark)
     mark = first1.send(mark)
-    mark = gate0.send(mark)
-    mark = gate1.send(mark)
+    own_rows = lax.dynamic_slice_in_dim(chained([tokens], mark)[0], me * depth, depth, 1)
+    own = [lax.dynamic_slice_in_dim(own_rows, (slot ^ k) * part, part, 0) for k in range(SLOTS)]
     shift_t, cum, fade, logs = step_sizes(place, tokens, dt_t, payloads, head_params.T, (mark,))
-    mark = first0.keep(cum)
-    mark = first1.keep(mark)
-    mark = gate0.keep(mark)
-    mark = gate1.keep(mark)
+    mark = gate0.keep(own[0], cum)
+    mark = gate1.keep(own[1], mark)
+    mark = first0.keep(jnp.concatenate([own[0], own_rows[tok_rows - EDGE :]], 0), mark)
+    mark = first1.keep(own[1], mark)
+    gates01 = finish("fin_gate", (gate0.total, gate1.total), (gate0.last, gate1.last), zx_scale[0:1], (mark,))
+    mark = gates01[0]
+    from_both = swapped(chained([from_chip], mark)[0], "head", 1)
+    first2, gate2 = (Reduction(blocks_of(from_chip), bits[::-1], w) for w in (first_w, gate_w))
+    first3, gate3 = (Reduction(blocks_of(from_both), bits, w) for w in (first_w, gate_w))
+    mark = first2.send(mark)
+    mark = first3.send(mark)
     scale = jnp.concatenate([zx_scale[1], pick_group(bc_scale, group_index, 0)], 0)[None]
     firsts01 = finish(
         "fin_first", (first0.total, first1.total), (first0.last, first1.last), scale, (mark,)
     )
     mark = firsts01[0]
     arrived = passed_along(firsts01[0][part:], "ctx", 1)
-    from_both = swapped(chained([from_chip], mark)[0], "head", 1)
-    first2, gate2 = quarter(2, blocks_of(from_chip))
-    first3, gate3 = quarter(3, blocks_of(from_both))
-    mark = first2.send(mark)
-    mark = first3.send(mark)
-    gates01 = finish("fin_gate", (gate0.total, gate1.total), (gate0.last, gate1.last), zx_scale[0:1], (mark,))
-    mark = gates01[0]
-    mark = first2.keep(mark)
-    mark = first3.keep(mark)
+    mark = first2.keep(own[2], mark)
+    mark = first3.keep(own[3], mark)
     mark = gate2.send(mark)
     mark = gate3.send(mark)
 
@@ -567,8 +561,8 @@
     conved, local_state = conv_and_state(
         place, firsts01, (first2.total, first3.total), (first2.last, first3.last), arrived, before, scale, taps, fade, logs, (mark,)
     )
-    mark = gate2.keep(conved)
-    mark = gate3.keep(mark)
+    mark = gate2.keep(own[2], conved)
+    mark = gate3.keep(own[3], mark)
     y_local = inner_output(conved, cum, shift_t, jnp.repeat(head_params[2], P_SIZE)[None], (mark,))
 
     run, gots = local_state, []

time: 184 us -> 180 us (0.978)
  matrix products: 37.5 us -> 45 us
  waiting for transfers between devices: 47 us -> 40.7 us
  other arithmetic: 4.38 us -> 0.86 us
  local copies, waits for them, and re-layouts: 34.9 us -> 32.5 us
    dot_general x24, matrix products: 37.5 us -> 45 us  [dot32(): return jnp.dot(a, b, preferred_element_type=F32)]
    ppermute x23, waiting for transfers between devices: 45 us -> 38.9 us  [swapped(): return lax.ppermute(x, axis, [(i, i ^ by) for i in range(length)])]
    unnamed x45 -> x43, local copies, waits for them, and re-layouts: 16.9 us -> 11.4 us
    concatenate x5 -> x4, other arithmetic: 3.75 us -> 0.26 us  [the longest x3 0.22 us: rows(): jnp.concatenate([self.blocks[j - 1] for j in offsets], 0)]
    squeeze x1, local copies, waits for them, and re-layouts: 2.51 us -> 5.53 us  [body(): first_w = jnp.concatenate([w_all[1], chained([bc_rows], mark)[0]], 1)]
    dynamic_slice x1, local copies, waits for them, and re-layouts: 3.69 us -> 1.1 us  [body(): lax.dynamic_slice_in_dim(own_rows, (slot ^ k) * part, part, 0)]
    concatenate x2, local copies, waits for them, and re-layouts: 0.17 us -> 2.74 us  [rows(): jnp.concatenate([self.blocks[j - 1] for j in offsets], 0)]
  transfers between devices with their start and end apart: 25 -> 25, of which waited for: 10 -> 8; matrix products, arithmetic and copies ran while one was open for 39% -> 44% of each run, Pallas kernels for 8% -> 8%
where the time goes in v1:
time: 180 us; the launch traced here: 177 us
  matrix products  45 us (25%)
  waiting for transfers between devices  40.7 us (23%)
  starting transfers between devices  33.9 us (19%)
  local copies, waits for them, and re-layouts  32.5 us (18%)
  Pallas kernels  23 us (13%)
    dot_general x24, matrix products, dot32(): return jnp.dot(a, b, preferred_element_type=F32)  45 us
    ppermute x23, waiting for transfers between devices, swapped(): return lax.ppermute(x, axis, [(i, i ^ by) for i in range(length)])  38.9 us
    ppermute x23, starting transfers between devices, swapped(): return lax.ppermute(x, axis, [(i, i ^ by) for i in range(length)])  27.2 us
    unnamed x43, local copies, waits for them, and re-layouts  11.4 us
    dynamic_slice x4, local copies, waits for them, and re-layouts, pick_group(): lax.dynamic_index_in_dim(values, group_index, axis_index, keepdims=False)  9.03 us
    ppermute x2, starting transfers between devices, passed_along(): return lax.ppermute(x, axis, pairs)  6.74 us
    squeeze x1, local copies, waits for them, and re-layouts, body(): first_w = jnp.concatenate([w_all[1], chained([bc_rows], mark)[0]], 1)  5.53 us
    pallas_call x1, Pallas kernels, conv_and_state(): pl.pallas_call(conv_kernel, in_specs=[SMEM] + [VMEM] * (2 * SLOTS - EARLY...  4.88 us
  transfers between devices with their start and end apart: 25, of which 8 were waited for; matrix products, arithmetic and copies ran while one was open for 44% of the time, Pallas kernels for 8%

profile of v1, /device:TPU:0, one launch (start us, length us, event | category | flops | bytes accessed | tf_op | source)
XLA Modules:
  0.0 176.8 jit_solution(5689451451086638439)
XLA Ops:
  0.6 3.4 %pack.1 = (bf16[160,2048]{1,0:T(8,128)(2,1)}, bf16[160,2048]{1,0:T(8,128)(2,1)}, bf16[160,2048]{1,0:T(8,128)(2,1)}) custom-call(s32[4]{0:T(128)} %pad_add_fusion.place_ref.me_ref, bf16[512,8192]{1,0:T(8,128)(2,1)} %tok_ref.1, bf16[512,8192]{1,0:T(8,128)(2,1)} %tok_ref.1, bf16[512,8192]{1,0:T(8,128)(2,1)} %tok_ref.1, bf16[512,8192]{1,0:T(8,128)(2,1)} %tok_ref.1, ...), custom_call_target="tpu_custom_call" | custom-call | tf_op jit(solution)/shard_map/pack/pallas_call | solution.py:85
  4.0 3.9 %collective-permute-start.2 = (bf16[160,2048]{1,0:T(8,128)(2,1)}, bf16[160,2048]{1,0:T(8,128)(2,1)S(1)}, u32[]{:S(2)}, u32[]{:S(2)}) collective-permute-start(bf16[160,2048]{1,0:T(8,128)(2,1)} %get-tuple-element.47), channel_id=1, source_target_pairs={{0,24},{8,16},{16,8},{24,0},{1,25},{9,17},{17,9},{25,1},{2,26},{10... | collective-permute-start | bytes 1966088 | tf_op jit(solution)/shard_map/ppermute | solution.py:56
  8.4 9.4 %copy.27 = bf16[2048,2,1024]{2,0,1:T(8,128)(2,1)} copy(bf16[2048,2,1024]{2,1,0:T(2,128)(2,1)} %param.14) | data formatting | bytes 16777216 | tf_op args[1]
  17.8 7.5 %constant_dynamic-slice_fusion.3 = bf16[2048,1,512]{2,1,0:T(2,128)(2,1)S(1)} fusion(bf16[2048,8,512]{2,1,0:T(8,128)(2,1)} %param.16, s32[]{:T(128)S(6)} %select_n.48), kind=kLoop, calls=%fused_computation.52 | loop fusion | bytes 4194308 | tf_op jit(solution)/shard_map/jit(dynamic_index_in_dim)/dynamic_slice | solution.py:60
  25.3 1.9 %copy.28 = bf16[2048,1,512]{2,0,1:T(8,128)(2,1)} copy(bf16[2048,1,512]{2,1,0:T(2,128)(2,1)S(1)} %constant_dynamic-slice_fusion.3) | data formatting | bytes 4194304
  28.9 5.5 %slice_bitcast_fusion = (bf16[2048,1024]{1,0:T(8,128)(2,1)}, bf16[2048,1024]{1,0:T(8,128)(2,1)S(1)}) fusion(bf16[2,2048,1024]{2,1,0:T(8,128)(2,1)} %bitcast.92), kind=kLoop, calls=%fused_computation.2 | loop fusion | bytes 16777216 | tf_op jit(solution)/shard_map/squeeze | solution.py:528
  34.4 2.7 %collective-permute-done.refs_0_.refs_1_ = bf16[160,2048]{1,0:T(8,128)(2,1)S(1)} collective-permute-done((bf16[160,2048]{1,0:T(8,128)(2,1)}, bf16[160,2048]{1,0:T(8,128)(2,1)S(1)}, u32[]{:S(2)}, u32[]{:S(2)}) %collective-permute-start) | collective-permute-done | bytes 655392 | tf_op jit(solution)/shard_map/ppermute | solution.py:56
  37.2 1.4 join.1
  38.7 1.6 collective-permute-start.12
  40.5 3.6 %convolution_convert_fusion.7 = bf16[256,1024]{1,0:T(8,128)(2,1)S(1)} fusion(bf16[256,2048]{1,0:T(8,128)(2,1)S(1)} %pad_maximum_fusion.2, bf16[2,2048,1024]{2,1,0:T(8,128)(2,1)} %bitcast.93), kind=kOutput, calls=%fused_computation.20 | convolution fusion | flops 1074003968 | bytes 5767168 | tf_op jit(solution)/shard_map/dot_general | solution.py:64
  44.1 1.6 collective-permute-start.4
  46.0 1.4 concatenate.43
  47.5 2.1 %convolution_convert_fusion.6 = bf16[256,1024]{1,0:T(8,128)(2,1)} fusion(bf16[256,2048]{1,0:T(8,128)(2,1)S(1)} %concatenate.43, bf16[2,2048,1024]{2,1,0:T(8,128)(2,1)S(1)} %bitcast.96), kind=kOutput, calls=%fused_computation.19 | convolution fusion | flops 1074003968 | bytes 5767168 | tf_op jit(solution)/shard_map/dot_general | solution.py:64
  49.5 1.4 collective-permute-start.5
  51.0 3.8 %convolution_convert_fusion = bf16[288,1536]{1,0:T(8,128)(2,1)} fusion(bf16[288,2048]{1,0:T(8,128)(2,1)S(1)} %pad_maximum_fusion.1, bf16[2048,512]{1,0:T(8,128)(2,1)S(1)} %bitcast.75, bf16[2048,1024]{1,0:T(8,128)(2,1)S(1)} %copy-done.9), kind=kOutput, calls=%fused_computation.4 | convolution fusion | flops 1824964608 | bytes 8355840 | tf_op jit(solution)/shard_map/dot_general | solution.py:64
  55.6 3.1 %convolution_convert_fusion.3.refs_5_ = bf16[256,1536]{1,0:T(8,128)(2,1)S(1)} fusion(bf16[256,2048]{1,0:T(8,128)(2,1)S(1)} %concatenate.43, bf16[2048,512]{1,0:T(8,128)(2,1)S(1)} %bitcast.76, bf16[2048,1024]{1,0:T(8,128)(2,1)S(1)} %copy-done.9), kind=kOutput, calls=%fused_computation.7 | convolution fusion | flops 1623588864 | bytes 8126464 | tf_op jit(solution)/shard_map/dot_general | solution.py:64
  59.4 4.8 %steps.1 = (f32[16,512]{1,0:T(8,128)S(1)}, f32[512,16]{1,0:T(8,128)S(1)}, f32[512,16]{1,0:T(8,128)S(1)}, f32[8,16]{1,0:T(8,128)S(1)}) custom-call(s32[4]{0:T(128)S(1)} %copy-done.7, bf16[512,8192]{1,0:T(8,128)(2,1)S(1)} %bitcast.73, bf16[16,2048]{1,0:T(8,128)(2,1)S(1)} %bitcast.89, bf16[160,2048]{1,0:T(8,128)(2,1)S(1)} %collective-permute-done.refs_0_.refs_1_, ...), custom_call_target="tpu_custom_call" | custom-call | flops 16777216 | bytes 131072 | tf_op jit(solution)/shard_map/steps/pallas_call | solution.py:236
  64.9 1.1 fusion.19
  66.0 1.5 collective-permute-start.6
  70.1 1.3 collective-permute-start.7
  72.1 6.0 %collective-permute-done.8 = bf16[288,1536]{1,0:T(8,128)(2,1)} collective-permute-done((bf16[288,1536]{1,0:T(8,128)(2,1)}, bf16[288,1536]{1,0:T(8,128)(2,1)}, u32[]{:S(2)}, u32[]{:S(2)}) %collective-permute-start.8) | collective-permute-done | bytes 884768 | tf_op jit(solution)/shard_map/ppermute | solution.py:56
  78.0 3.8 %fusion = bf16[144,1536]{1,0:T(8,128)(2,1)S(1)} fusion(bf16[144,2048]{1,0:T(8,128)(2,1)S(1)} %slice-done.2, bf16[288,1536]{1,0:T(8,128)(2,1)} %collective-permute-done.8, bf16[2048,512]{1,0:T(8,128)(2,1)S(1)} %bitcast.77, bf16[2048,1024]{1,0:T(8,128)(2,1)S(1)} %copy-done.10), kind=kOutput, calls=%fused_computation.12 | convolution fusion | flops 919216128 | bytes 7766016 | tf_op jit(solution)/shard_map/dot_general | solution.py:64
  81.9 2.9 %fusion.1.refs_5_ = bf16[128,1536]{1,0:T(8,128)(2,1)S(1)} fusion(bf16[128,2048]{1,0:T(8,128)(2,1)S(1)} %slice.162, bf16[256,1536]{1,0:T(8,128)(2,1)S(1)} %collective-permute-done.9, bf16[2048,512]{1,0:T(8,128)(2,1)S(1)} %bitcast.78, bf16[2048,1024]{1,0:T(8,128)(2,1)S(1)} %copy-done.10), kind=kOutput, calls=%fused_computation.13 | convolution fusion | flops 818479104 | bytes 7602176 | tf_op jit(solution)/shard_map/dot_general | solution.py:64
  84.7 1.2 collective-permute-done.6.refs_2_
  86.3 1.3 concatenate.44
  88.7 1.5 collective-permute-start.10
  91.1 3.1 %convolution_convert_fusion.2 = bf16[256,1536]{1,0:T(8,128)(2,1)S(1)} fusion(bf16[256,2048]{1,0:T(8,128)(2,1)S(1)} %concatenate.44, bf16[2048,512]{1,0:T(8,128)(2,1)S(1)} %bitcast.79, bf16[2048,1024]{1,0:T(8,128)(2,1)S(1)} %copy-done.10), kind=kOutput, calls=%fused_computation.6 | convolution fusion | flops 1623588864 | bytes 8126464 | tf_op jit(solution)/shard_map/dot_general | solution.py:64
  95.9 2.1 %convert_add_fusion.refs_0_ = f32[144,1536]{1,0:T(8,128)S(1)} fusion(bf16[288,1536]{1,0:T(8,128)(2,1)} %collective-permute-done.8, bf16[144,2048]{1,0:T(8,128)(2,1)S(1)} %pad_maximum_fusion.4, bf16[2048,512]{1,0:T(8,128)(2,1)S(1)} %bitcast.81, bf16[2048,1024]{1,0:T(8,128)(2,1)S(1)} %copy-done.10), kind=kOutput, calls=%fused_computation.32 | convolution fusion | flops 918994944 | bytes 8208384 | tf_op jit(solution)/shard_map/dot_general | solution.py:64
  98.3 3.1 %convolution_convert_fusion.1.refs_5_ = bf16[256,1536]{1,0:T(8,128)(2,1)S(1)} fusion(bf16[256,2048]{1,0:T(8,128)(2,1)S(1)} %pad_maximum_fusion.3, bf16[2048,512]{1,0:T(8,128)(2,1)S(1)} %bitcast.82, bf16[2048,1024]{1,0:T(8,128)(2,1)S(1)} %copy-done.10), kind=kOutput, calls=%fused_computation.5 | convolution fusion | flops 1623588864 | bytes 8126464 | tf_op jit(solution)/shard_map/dot_general | solution.py:64
  101.4 1.1 collective-permute-start.15
  102.7 15.4 %collective-permute-done.14 = bf16[256,1536]{1,0:T(8,128)(2,1)S(1)} collective-permute-done((bf16[256,1536]{1,0:T(8,128)(2,1)S(1)}, bf16[256,1536]{1,0:T(8,128)(2,1)S(1)}, u32[]{:S(2)}, u32[]{:S(2)}) %collective-permute-start.14) | collective-permute-done | bytes 786464 | tf_op jit(solution)/shard_map/ppermute | solution.py:56
  118.1 3.2 %fusion.2 = bf16[128,1536]{1,0:T(8,128)(2,1)S(1)} fusion(bf16[128,2048]{1,0:T(8,128)(2,1)S(1)} %slice.172, bf16[256,1536]{1,0:T(8,128)(2,1)S(1)} %collective-permute-done.14, bf16[2048,512]{1,0:T(8,128)(2,1)S(1)} %bitcast.83, bf16[2048,1024]{1,0:T(8,128)(2,1)S(1)} %copy-done.10), kind=kOutput, calls=%fused_computation.14 | convolution fusion | flops 818479104 | bytes 7602176 | tf_op jit(solution)/shard_map/dot_general | solution.py:64
  122.4 3.0 %collective-permute-start.18 = (bf16[16,1536]{1,0:T(8,128)(2,1)S(1)}, bf16[16,1536]{1,0:T(8,128)(2,1)S(1)}, u32[]{:S(2)}, u32[]{:S(2)}) collective-permute-start(bf16[16,1536]{1,0:T(8,128)(2,1)S(1)} %slice.146), channel_id=1, source_target_pairs={{0,8},{8,16},{16,24},{1,9},{9,17},{17,25},{2,10},{10,18},{18,26},{... | collective-permute-start | bytes 147464 | tf_op jit(solution)/shard_map/ppermute | solution.py:51
  126.4 2.9 %fusion.3 = bf16[128,1536]{1,0:T(8,128)(2,1)S(1)} fusion(bf16[128,2048]{1,0:T(8,128)(2,1)S(1)} %get-tuple-element.82, bf16[256,1536]{1,0:T(8,128)(2,1)S(1)} %collective-permute-done.15, bf16[2048,512]{1,0:T(8,128)(2,1)S(1)} %bitcast.85, bf16[2048,1024]{1,0:T(8,128)(2,1)S(1)} %copy-done.10), kind=kOutput, calls=%fused_computation.15 | convolution fusion | flops 818479104 | bytes 7602176 | tf_op jit(solution)/shard_map/dot_general | solution.py:64
  129.3 1.5 collective-permute-start.17
  130.7 1.2 convolution_convert_fusion.5
  132.7 1.2 convolution_convert_fusion.4.refs_12_
  133.9 1.9 %collective-permute-start.20 = (bf16[256,1024]{1,0:T(8,128)(2,1)S(1)}, bf16[256,1024]{1,0:T(8,128)(2,1)S(1)}, u32[]{:S(2)}, u32[]{:S(2)}) collective-permute-start(bf16[256,1024]{1,0:T(8,128)(2,1)S(1)} %convolution_convert_fusion.4.refs_12_), channel_id=1, source_target_pairs={{0,8},{8,0},{16,24},{24,16},{1,9},{9,1},{17,25},{25,17},{2,10},{10... | collective-permute-start | bytes 1572872 | tf_op jit(solution)/shard_map/ppermute | solution.py:56
  136.9 4.5 %collective-permute-done.17.refs_5_ = bf16[128,1536]{1,0:T(8,128)(2,1)S(1)} collective-permute-done((bf16[128,1536]{1,0:T(8,128)(2,1)S(1)}, bf16[128,1536]{1,0:T(8,128)(2,1)S(1)}, u32[]{:S(2)}, u32[]{:S(2)}) %collective-permute-start.17) | collective-permute-done | bytes 393248 | tf_op jit(solution)/shard_map/ppermute | solution.py:56
  141.4 4.9 %conv.1 = (bf16[512,1536]{1,0:T(8,128)(2,1)S(1)}, bf16[272,1024]{1,0:T(8,128)(2,1)S(1)}) custom-call(s32[4]{0:T(128)S(1)} %copy-done.7, bf16[144,1536]{1,0:T(8,128)(2,1)S(1)} %get-tuple-element.68.refs_0_, bf16[128,1536]{1,0:T(8,128)(2,1)S(1)} %get-tuple-element.69.refs_1_, f32[128,1536]{1,0:T(8,128)S(1)} %convert_add_fusion.2.refs_2_, ...), custom_call_target="tpu_custom_call" | custom-call | flops 368640 | bytes 147456 | tf_op jit(solution)/shard_map/conv/pallas_call | solution.py:344
  146.3 1.9 %collective-permute-start.23 = (bf16[272,1024]{1,0:T(8,128)(2,1)S(1)}, bf16[272,1024]{1,0:T(8,128)(2,1)S(1)}, u32[]{:S(2)}, u32[]{:S(2)}) collective-permute-start(bf16[272,1024]{1,0:T(8,128)(2,1)S(1)} %get-tuple-element.83.own_ref), channel_id=1, source_target_pairs={{0,8},{8,0},{16,24},{24,16},{1,9},{9,1},{17,25},{25,17},{2,10},{10... | collective-permute-start | bytes 1671176 | tf_op jit(solution)/shard_map/ppermute | solution.py:56
  148.2 2.6 %collective-permute-done.19 = bf16[256,1024]{1,0:T(8,128)(2,1)S(1)} collective-permute-done((bf16[256,1024]{1,0:T(8,128)(2,1)S(1)}, bf16[256,1024]{1,0:T(8,128)(2,1)S(1)}, u32[]{:S(2)}, u32[]{:S(2)}) %collective-permute-start.19) | collective-permute-done | bytes 524320 | tf_op jit(solution)/shard_map/ppermute | solution.py:56
  151.5 1.9 %collective-permute-start.21 = (bf16[128,1024]{1,0:T(8,128)(2,1)S(1)}, bf16[128,1024]{1,0:T(8,128)(2,1)S(1)}, u32[]{:S(2)}, u32[]{:S(2)}) collective-permute-start(bf16[128,1024]{1,0:T(8,128)(2,1)S(1)} %fusion.6), channel_id=1, source_target_pairs={{0,8},{8,0},{16,24},{24,16},{1,9},{9,1},{17,25},{25,17},{2,10},{10... | collective-permute-start | bytes 786440 | tf_op jit(solution)/shard_map/ppermute | solution.py:56
  154.7 6.5 %collective-permute-done.23.got_ref.refs_6_ = bf16[272,1024]{1,0:T(8,128)(2,1)S(1)} collective-permute-done((bf16[272,1024]{1,0:T(8,128)(2,1)S(1)}, bf16[272,1024]{1,0:T(8,128)(2,1)S(1)}, u32[]{:S(2)}, u32[]{:S(2)}) %collective-permute-start.23) | collective-permute-done | bytes 557088 | tf_op jit(solution)/shard_map/ppermute | solution.py:56
  162.0 3.8 %collective-permute-start.24 = (bf16[272,1024]{1,0:T(8,128)(2,1)S(1)}, bf16[272,1024]{1,0:T(8,128)(2,1)S(1)}, u32[]{:S(2)}, u32[]{:S(2)}) collective-permute-start(bf16[272,1024]{1,0:T(8,128)(2,1)S(1)} %merge.1), channel_id=1, source_target_pairs={{0,16},{8,24},{1,17},{9,25},{2,18},{10,26},{3,19},{11,27},{4,20},{... | collective-permute-start | bytes 1671176 | tf_op jit(solution)/shard_map/ppermute | solution.py:51
  166.6 3.5 %inner.1.refs_8_ = f32[512,1024]{1,0:T(8,128)S(1)} custom-call(bf16[512,1536]{1,0:T(8,128)(2,1)S(1)} %get-tuple-element.78.conv_ref.refs_9_, f32[512,16]{1,0:T(8,128)S(1)} %get-tuple-element.54.cum_ref.refs_11_, f32[16,512]{1,0:T(8,128)S(1)} %get-tuple-element.84.shift_t_ref, f32[1,1024]{1,0:T(1,128)S(1)} %broadcast_in_dim_reshape.3.skip_ref, ...), custom_call_target="tpu_custom_call" | custom-call | flops 8388608 | bytes 98304 | tf_op jit(solution)/shard_map/inner/pallas_call | solution.py:392
  170.9 1.8 %collective-permute-done.24.refs_7_ = bf16[272,1024]{1,0:T(8,128)(2,1)S(1)} collective-permute-done((bf16[272,1024]{1,0:T(8,128)(2,1)S(1)}, bf16[272,1024]{1,0:T(8,128)(2,1)S(1)}, u32[]{:S(2)}, u32[]{:S(2)}) %collective-permute-start.24) | collective-permute-done | bytes 557088 | tf_op jit(solution)/shard_map/ppermute | solution.py:51
  172.6 4.0 %final.1 = bf16[512,1024]{1,0:T(8,128)(2,1)} custom-call(s32[4]{0:T(128)S(1)} %copy-done.7, bf16[128,1024]{1,0:T(8,128)(2,1)S(1)} %get-tuple-element.61.refs_0_, bf16[128,1024]{1,0:T(8,128)(2,1)S(1)} %get-tuple-element.62.refs_1_, f32[128,1024]{1,0:T(8,128)S(1)} %convert_add_fusion.5.refs_2_, f32[128,1024]{1,0:T(8,128)S(1)} %convert_add_fusion.4.refs_3_, ...), custom_call_target="tpu_custom_call" | custom-call | flops 4194304 | bytes 98304 | tf_op jit(solution)/shard_map/final/pallas_call | solution.py:468
  (114 shorter events, 21.3 us)
Async XLA Ops:
  0.0 28.8 %copy-start = (f32[5,8,512]{2,1,0:T(8,128)S(1)}, f32[5,8,512]{2,1,0:T(8,128)}, u32[]{:S(2)}) copy-start(f32[5,8,512]{2,1,0:T(8,128)} %param.20) | copy-start | bytes 245764
  4.0 30.5 %collective-permute-start.2 = (bf16[160,2048]{1,0:T(8,128)(2,1)}, bf16[160,2048]{1,0:T(8,128)(2,1)S(1)}, u32[]{:S(2)}, u32[]{:S(2)}) collective-permute-start(bf16[160,2048]{1,0:T(8,128)(2,1)} %get-tuple-element.47), channel_id=1, source_target_pairs={{0,24},{8,16},{16,8},{24,0},{1,25},{9,17},{17,9},{25,1},{2,26},{10... | collective-permute-start | bytes 1966088 | tf_op jit(solution)/shard_map/ppermute | solution.py:56
  7.9 29.3 %collective-permute-start = (bf16[160,2048]{1,0:T(8,128)(2,1)}, bf16[160,2048]{1,0:T(8,128)(2,1)S(1)}, u32[]{:S(2)}, u32[]{:S(2)}) collective-permute-start(bf16[160,2048]{1,0:T(8,128)(2,1)} %get-tuple-element.45), channel_id=1, source_target_pairs={{0,8},{8,0},{16,24},{24,16},{1,9},{9,1},{17,25},{25,17},{2,10},{10... | collective-permute-start | bytes 1966088 | tf_op jit(solution)/shard_map/ppermute | solution.py:56
  8.4 28.7 %collective-permute-start.1 = (bf16[160,2048]{1,0:T(8,128)(2,1)}, bf16[160,2048]{1,0:T(8,128)(2,1)S(1)}, u32[]{:S(2)}, u32[]{:S(2)}) collective-permute-start(bf16[160,2048]{1,0:T(8,128)(2,1)} %get-tuple-element.46), channel_id=1, source_target_pairs={{0,16},{8,24},{16,0},{24,8},{1,17},{9,25},{17,1},{25,9},{2,18},{10... | collective-permute-start | bytes 1966088 | tf_op jit(solution)/shard_map/ppermute | solution.py:56
  17.8 9.4 %copy-start.14 = (f32[3,16]{1,0:T(4,128)S(1)}, f32[3,16]{1,0:T(4,128)}, u32[]{:S(2)}) copy-start(f32[3,16]{1,0:T(4,128)} %param.23) | copy-start | bytes 580
  17.8 9.5 %copy-start.13 = (f32[2,1024]{1,0:T(2,128)S(1)}, f32[2,1024]{1,0:T(2,128)}, u32[]{:S(2)}) copy-start(f32[2,1024]{1,0:T(2,128)} %param.15) | copy-start | bytes 24580
  28.9 8.3 %copy-start.3 = (bf16[2048,1,512]{2,0,1:T(8,128)(2,1)S(1)}, bf16[2048,1,512]{2,0,1:T(8,128)(2,1)}, u32[]{:S(2)}) copy-start(bf16[2048,1,512]{2,0,1:T(8,128)(2,1)} %copy.28) | copy-start | bytes 6291460
  34.4 4.3 %copy-start.12 = (bf16[3,1024]{1,0:T(4,128)(2,1)S(1)}, bf16[3,1024]{1,0:T(4,128)(2,1)}, u32[]{:S(2)}) copy-start(bf16[3,1024]{1,0:T(4,128)(2,1)} %param.21) | copy-start | bytes 18436
  34.4 4.3 %copy-start.11 = (f32[5,1024]{1,0:T(8,128)S(1)}, f32[5,1024]{1,0:T(8,128)}, u32[]{:S(2)}) copy-start(f32[5,1024]{1,0:T(8,128)} %param.19) | copy-start | bytes 61444
  37.1 22.2 %copy-start.2 = (bf16[160,2048]{1,0:T(8,128)(2,1)}, bf16[160,2048]{1,0:T(8,128)(2,1)S(1)}, u32[]{:S(2)}) copy-start(bf16[160,2048]{1,0:T(8,128)(2,1)S(1)} %collective-permute-done.1.refs_1_.refs_2_) | copy-start | bytes 1966084
  38.5 7.4 %collective-permute-start.3 = (bf16[384,2048]{1,0:T(8,128)(2,1)}, bf16[384,2048]{1,0:T(8,128)(2,1)}, u32[]{:S(2)}, u32[]{:S(2)}) collective-permute-start(bf16[384,2048]{1,0:T(8,128)(2,1)} %join.1), channel_id=1, source_target_pairs={{0,1},{1,0},{2,3},{3,2},{4,5},{5,4},{6,7},{7,6},{8,9},{9,8},{10,11... | collective-permute-start | bytes 4718600 | tf_op jit(solution)/shard_map/ppermute | solution.py:56
  38.7 47.4 %collective-permute-start.12 = (bf16[384,2048]{1,0:T(8,128)(2,1)}, bf16[384,2048]{1,0:T(8,128)(2,1)}, u32[]{:S(2)}, u32[]{:S(2)}) collective-permute-start(bf16[384,2048]{1,0:T(8,128)(2,1)} %join.1), channel_id=1, source_target_pairs={{0,2},{1,3},{2,0},{3,1},{4,6},{5,7},{6,4},{7,5},{8,10},{9,11},{10,... | collective-permute-start | bytes 4718600 | tf_op jit(solution)/shard_map/ppermute | solution.py:56
  40.5 6.9 %slice-start.3 = ((s8[8388608]{0:T(1024)(128)(4,1)}), s8[4194304]{0:T(1024)(128)(4,1)S(1)}, s32[]{:S(2)}) async-start(s8[8388608]{0:T(1024)(128)(4,1)} %bitcast.94), calls=%async_computation.4 | async-start | bytes 8388608
  44.1 3.3 %slice-start.4 = ((s8[8388608]{0:T(1024)(128)(4,1)}), s8[4194304]{0:T(1024)(128)(4,1)S(1)}, s32[]{:S(2)}) async-start(s8[8388608]{0:T(1024)(128)(4,1)} %bitcast.94), calls=%async_computation.5 | async-start | bytes 8388608
  44.1 20.0 %collective-permute-start.4 = (bf16[256,1024]{1,0:T(8,128)(2,1)S(1)}, bf16[256,1024]{1,0:T(8,128)(2,1)S(1)}, u32[]{:S(2)}, u32[]{:S(2)}) collective-permute-start(bf16[256,1024]{1,0:T(8,128)(2,1)S(1)} %convolution_convert_fusion.7), channel_id=1, source_target_pairs={{0,8},{8,0},{16,24},{24,16},{1,9},{9,1},{17,25},{25,17},{2,10},{10... | collective-permute-start | bytes 1572872 | tf_op jit(solution)/shard_map/ppermute | solution.py:56
  45.8 5.1 %copy-start.4 = (bf16[2048,1,512]{2,0,1:T(8,128)(2,1)S(1)}, bf16[2048,1,512]{2,0,1:T(8,128)(2,1)}, u32[]{:S(2)}) copy-start(bf16[2048,1,512]{2,0,1:T(8,128)(2,1)} %copy.28) | copy-start | bytes 6291460
  45.9 5.1 %copy-start.9 = (bf16[2048,1024]{1,0:T(8,128)(2,1)S(1)}, bf16[2048,1024]{1,0:T(8,128)(2,1)}, u32[]{:S(2)}) copy-start(bf16[2048,1024]{1,0:T(8,128)(2,1)} %get-tuple-element.89) | copy-start | bytes 12582916
  47.4 11.9 %slice-start = ((s8[8388608]{0:T(1024)(128)(4,1)}), s8[4194304]{0:T(1024)(128)(4,1)S(1)}, s32[]{:S(2)}) async-start(s8[8388608]{0:T(1024)(128)(4,1)} %bitcast.72), calls=%async_computation | async-start | bytes 8388608
  49.5 19.8 %collective-permute-start.5 = (bf16[256,1024]{1,0:T(8,128)(2,1)}, bf16[256,1024]{1,0:T(8,128)(2,1)S(1)}, u32[]{:S(2)}, u32[]{:S(2)}) collective-permute-start(bf16[256,1024]{1,0:T(8,128)(2,1)} %convolution_convert_fusion.6), channel_id=1, source_target_pairs={{0,16},{8,24},{16,0},{24,8},{1,17},{9,25},{17,1},{25,9},{2,18},{10... | collective-permute-start | bytes 1572872 | tf_op jit(solution)/shard_map/ppermute | solution.py:56
  51.0 8.4 %slice-start.1 = ((s8[8388608]{0:T(1024)(128)(4,1)}), s8[4194304]{0:T(1024)(128)(4,1)S(1)}, s32[]{:S(2)}) async-start(s8[8388608]{0:T(1024)(128)(4,1)} %bitcast.72), calls=%async_computation.1 | async-start | bytes 8388608
  54.8 4.6 %copy-start.6 = (bf16[2048,16]{0,1:T(8,128)(2,1)S(1)}, bf16[2048,16]{0,1:T(8,128)(2,1)}, u32[]{:S(2)}) copy-start(bf16[2048,16]{0,1:T(8,128)(2,1)} %param.18) | copy-start | bytes 196612
  54.8 4.6 %copy-start.7 = (s32[4]{0:T(128)S(1)}, s32[4]{0:T(128)}, u32[]{:S(2)}) copy-start(s32[4]{0:T(128)} %pad_add_fusion.place_ref.me_ref) | copy-start | bytes 52
  54.8 23.3 %collective-permute-start.8 = (bf16[288,1536]{1,0:T(8,128)(2,1)}, bf16[288,1536]{1,0:T(8,128)(2,1)}, u32[]{:S(2)}, u32[]{:S(2)}) collective-permute-start(bf16[288,1536]{1,0:T(8,128)(2,1)} %convolution_convert_fusion), channel_id=1, source_target_pairs={{0,8},{8,0},{16,24},{24,16},{1,9},{9,1},{17,25},{25,17},{2,10},{10... | collective-permute-start | bytes 2654216 | tf_op jit(solution)/shard_map/ppermute | solution.py:56
  58.7 23.2 %collective-permute-start.9 = (bf16[256,1536]{1,0:T(8,128)(2,1)S(1)}, bf16[256,1536]{1,0:T(8,128)(2,1)S(1)}, u32[]{:S(2)}, u32[]{:S(2)}) collective-permute-start(bf16[256,1536]{1,0:T(8,128)(2,1)S(1)} %convolution_convert_fusion.3.refs_5_), channel_id=1, source_target_pairs={{0,16},{8,24},{16,0},{24,8},{1,17},{9,25},{17,1},{25,9},{2,18},{10... | collective-permute-start | bytes 2359304 | tf_op jit(solution)/shard_map/ppermute | solution.py:56
  66.0 20.0 %collective-permute-start.6 = (bf16[128,1024]{1,0:T(8,128)(2,1)S(1)}, bf16[128,1024]{1,0:T(8,128)(2,1)S(1)}, u32[]{:S(2)}, u32[]{:S(2)}) collective-permute-start(bf16[128,1024]{1,0:T(8,128)(2,1)S(1)} %fusion.4), channel_id=1, source_target_pairs={{0,16},{8,24},{16,0},{24,8},{1,17},{9,25},{17,1},{25,9},{2,18},{10... | collective-permute-start | bytes 786440 | tf_op jit(solution)/shard_map/ppermute | solution.py:56
  69.3 8.7 %slice-start.2 = ((bf16[160,2048]{1,0:T(8,128)(2,1)}), bf16[144,2048]{1,0:T(8,128)(2,1)S(1)}, s32[]{:S(2)}) async-start(bf16[160,2048]{1,0:T(8,128)(2,1)} %copy-done.2), calls=%async_computation.3 | async-start | bytes 1179648 | tf_op jit(solution)/shard_map/slice | solution.py:529
  69.3 8.7 %copy-start.10 = (bf16[2048,1024]{1,0:T(8,128)(2,1)S(1)}, bf16[2048,1024]{1,0:T(8,128)(2,1)}, u32[]{:S(2)}) copy-start(bf16[2048,1024]{1,0:T(8,128)(2,1)} %get-tuple-element.89) | copy-start | bytes 12582916
  70.1 15.9 %collective-permute-start.7 = (bf16[128,1024]{1,0:T(8,128)(2,1)S(1)}, bf16[128,1024]{1,0:T(8,128)(2,1)S(1)}, u32[]{:S(2)}, u32[]{:S(2)}) collective-permute-start(bf16[128,1024]{1,0:T(8,128)(2,1)S(1)} %fusion.5), channel_id=1, source_target_pairs={{0,8},{8,0},{16,24},{24,16},{1,9},{9,1},{17,25},{25,17},{2,10},{10... | collective-permute-start | bytes 786440 | tf_op jit(solution)/shard_map/ppermute | solution.py:56
  81.8 4.4 %dynamic-slice-start = ((bf16[512,8192]{1,0:T(8,128)(2,1)}, s32[]{:T(128)}, s32[]{:T(128)}), bf16[16,2048]{1,0:T(8,128)(2,1)S(1)}, s32[]{:S(2)}) async-start(bf16[512,8192]{1,0:T(8,128)(2,1)} %tok_ref.1, s32[]{:T(128)} %add.114, s32[]{:T(128)} %select_n.51), calls=%async_computation.2 | async-start | bytes 131584 | tf_op jit(solution)/shard_map/slice | solution.py:538
  86.1 11.9 %collective-permute-start.13 = (bf16[384,2048]{1,0:T(8,128)(2,1)}, bf16[384,2048]{1,0:T(8,128)(2,1)S(1)}, u32[]{:S(2)}, u32[]{:S(2)}) collective-permute-start(bf16[384,2048]{1,0:T(8,128)(2,1)} %collective-permute-done.12), channel_id=1, source_target_pairs={{0,1},{1,0},{2,3},{3,2},{4,5},{5,4},{6,7},{7,6},{8,9},{9,8},{10,11... | collective-permute-start | bytes 4718600 | tf_op jit(solution)/shard_map/ppermute | solution.py:56
  88.7 13.9 %collective-permute-start.10 = (bf16[144,1536]{1,0:T(8,128)(2,1)S(1)}, bf16[144,1536]{1,0:T(8,128)(2,1)S(1)}, u32[]{:S(2)}, u32[]{:S(2)}) collective-permute-start(bf16[144,1536]{1,0:T(8,128)(2,1)S(1)} %fusion), channel_id=1, source_target_pairs={{0,16},{8,24},{16,0},{24,8},{1,17},{9,25},{17,1},{25,9},{2,18},{10... | collective-permute-start | bytes 1327112 | tf_op jit(solution)/shard_map/ppermute | solution.py:56
  90.1 12.4 %collective-permute-start.11 = (bf16[128,1536]{1,0:T(8,128)(2,1)S(1)}, bf16[128,1536]{1,0:T(8,128)(2,1)S(1)}, u32[]{:S(2)}, u32[]{:S(2)}) collective-permute-start(bf16[128,1536]{1,0:T(8,128)(2,1)S(1)} %fusion.1.refs_5_), channel_id=1, source_target_pairs={{0,8},{8,0},{16,24},{24,16},{1,9},{9,1},{17,25},{25,17},{2,10},{10... | collective-permute-start | bytes 1179656 | tf_op jit(solution)/shard_map/ppermute | solution.py:56
  94.2 23.9 %collective-permute-start.14 = (bf16[256,1536]{1,0:T(8,128)(2,1)S(1)}, bf16[256,1536]{1,0:T(8,128)(2,1)S(1)}, u32[]{:S(2)}, u32[]{:S(2)}) collective-permute-start(bf16[256,1536]{1,0:T(8,128)(2,1)S(1)} %convolution_convert_fusion.2), channel_id=1, source_target_pairs={{0,16},{8,24},{16,0},{24,8},{1,17},{9,25},{17,1},{25,9},{2,18},{10... | collective-permute-start | bytes 2359304 | tf_op jit(solution)/shard_map/ppermute | solution.py:56
  101.4 25.0 %collective-permute-start.15 = (bf16[256,1536]{1,0:T(8,128)(2,1)S(1)}, bf16[256,1536]{1,0:T(8,128)(2,1)S(1)}, u32[]{:S(2)}, u32[]{:S(2)}) collective-permute-start(bf16[256,1536]{1,0:T(8,128)(2,1)S(1)} %convolution_convert_fusion.1.refs_5_), channel_id=1, source_target_pairs={{0,8},{8,0},{16,24},{24,16},{1,9},{9,1},{17,25},{25,17},{2,10},{10... | collective-permute-start | bytes 2359304 | tf_op jit(solution)/shard_map/ppermute | solution.py:56
  121.4 15.5 %collective-permute-start.16 = (bf16[128,1536]{1,0:T(8,128)(2,1)S(1)}, bf16[128,1536]{1,0:T(8,128)(2,1)S(1)}, u32[]{:S(2)}, u32[]{:S(2)}) collective-permute-start(bf16[128,1536]{1,0:T(8,128)(2,1)S(1)} %fusion.2), channel_id=1, source_target_pairs={{0,8},{8,0},{16,24},{24,16},{1,9},{9,1},{17,25},{25,17},{2,10},{10... | collective-permute-start | bytes 1179656 | tf_op jit(solution)/shard_map/ppermute | solution.py:56
  122.4 14.5 %collective-permute-start.18 = (bf16[16,1536]{1,0:T(8,128)(2,1)S(1)}, bf16[16,1536]{1,0:T(8,128)(2,1)S(1)}, u32[]{:S(2)}, u32[]{:S(2)}) collective-permute-start(bf16[16,1536]{1,0:T(8,128)(2,1)S(1)} %slice.146), channel_id=1, source_target_pairs={{0,8},{8,16},{16,24},{1,9},{9,17},{17,25},{2,10},{10,18},{18,26},{... | collective-permute-start | bytes 147464 | tf_op jit(solution)/shard_map/ppermute | solution.py:51
  129.3 12.1 %collective-permute-start.17 = (bf16[128,1536]{1,0:T(8,128)(2,1)S(1)}, bf16[128,1536]{1,0:T(8,128)(2,1)S(1)}, u32[]{:S(2)}, u32[]{:S(2)}) collective-permute-start(bf16[128,1536]{1,0:T(8,128)(2,1)S(1)} %fusion.3), channel_id=1, source_target_pairs={{0,16},{8,24},{16,0},{24,8},{1,17},{9,25},{17,1},{25,9},{2,18},{10... | collective-permute-start | bytes 1179656 | tf_op jit(solution)/shard_map/ppermute | solution.py:56
  132.0 18.7 %collective-permute-start.19 = (bf16[256,1024]{1,0:T(8,128)(2,1)S(1)}, bf16[256,1024]{1,0:T(8,128)(2,1)S(1)}, u32[]{:S(2)}, u32[]{:S(2)}) collective-permute-start(bf16[256,1024]{1,0:T(8,128)(2,1)S(1)} %convolution_convert_fusion.5), channel_id=1, source_target_pairs={{0,16},{8,24},{16,0},{24,8},{1,17},{9,25},{17,1},{25,9},{2,18},{10... | collective-permute-start | bytes 1572872 | tf_op jit(solution)/shard_map/ppermute | solution.py:56
  133.9 19.4 %collective-permute-start.20 = (bf16[256,1024]{1,0:T(8,128)(2,1)S(1)}, bf16[256,1024]{1,0:T(8,128)(2,1)S(1)}, u32[]{:S(2)}, u32[]{:S(2)}) collective-permute-start(bf16[256,1024]{1,0:T(8,128)(2,1)S(1)} %convolution_convert_fusion.4.refs_12_), channel_id=1, source_target_pairs={{0,8},{8,0},{16,24},{24,16},{1,9},{9,1},{17,25},{25,17},{2,10},{10... | collective-permute-start | bytes 1572872 | tf_op jit(solution)/shard_map/ppermute | solution.py:56
  146.3 15.0 %collective-permute-start.23 = (bf16[272,1024]{1,0:T(8,128)(2,1)S(1)}, bf16[272,1024]{1,0:T(8,128)(2,1)S(1)}, u32[]{:S(2)}, u32[]{:S(2)}) collective-permute-start(bf16[272,1024]{1,0:T(8,128)(2,1)S(1)} %get-tuple-element.83.own_ref), channel_id=1, source_target_pairs={{0,8},{8,0},{16,24},{24,16},{1,9},{9,1},{17,25},{25,17},{2,10},{10... | collective-permute-start | bytes 1671176 | tf_op jit(solution)/shard_map/ppermute | solution.py:56
  151.5 19.4 %collective-permute-start.21 = (bf16[128,1024]{1,0:T(8,128)(2,1)S(1)}, bf16[128,1024]{1,0:T(8,128)(2,1)S(1)}, u32[]{:S(2)}, u32[]{:S(2)}) collective-permute-start(bf16[128,1024]{1,0:T(8,128)(2,1)S(1)} %fusion.6), channel_id=1, source_target_pairs={{0,8},{8,0},{16,24},{24,16},{1,9},{9,1},{17,25},{25,17},{2,10},{10... | collective-permute-start | bytes 786440 | tf_op jit(solution)/shard_map/ppermute | solution.py:56
  154.1 16.8 %collective-permute-start.22 = (bf16[128,1024]{1,0:T(8,128)(2,1)S(1)}, bf16[128,1024]{1,0:T(8,128)(2,1)S(1)}, u32[]{:S(2)}, u32[]{:S(2)}) collective-permute-start(bf16[128,1024]{1,0:T(8,128)(2,1)S(1)} %fusion.7.refs_0_), channel_id=1, source_target_pairs={{0,16},{8,24},{16,0},{24,8},{1,17},{9,25},{17,1},{25,9},{2,18},{10... | collective-permute-start | bytes 786440 | tf_op jit(solution)/shard_map/ppermute | solution.py:56
  162.0 10.6 %collective-permute-start.24 = (bf16[272,1024]{1,0:T(8,128)(2,1)S(1)}, bf16[272,1024]{1,0:T(8,128)(2,1)S(1)}, u32[]{:S(2)}, u32[]{:S(2)}) collective-permute-start(bf16[272,1024]{1,0:T(8,128)(2,1)S(1)} %merge.1), channel_id=1, source_target_pairs={{0,16},{8,24},{1,17},{9,25},{2,18},{10,26},{3,19},{11,27},{4,20},{... | collective-permute-start | bytes 1671176 | tf_op jit(solution)/shard_map/ppermute | solution.py:51
  166.5 6.1 %copy-start.5 = (f32[16,64,256]{2,1,0:T(8,128)S(1)}, f32[16,64,256]{2,1,0:T(8,128)}, u32[]{:S(2)}) copy-start(f32[16,64,256]{2,1,0:T(8,128)} %param.24) | copy-start | bytes 3145732
  166.6 6.1 %copy-start.8 = (f32[1024]{0:T(1024)S(1)}, f32[1024]{0:T(1024)}, u32[]{:S(2)}) copy-start(f32[1024]{0:T(1024)} %param.25) | copy-start | bytes 12292
  166.6 10.1 %copy-start.1 = (f32[5,8,512]{2,1,0:T(8,128)S(1)}, f32[5,8,512]{2,1,0:T(8,128)}, u32[]{:S(2)}) copy-start(f32[5,8,512]{2,1,0:T(8,128)} %param.20) | copy-start | bytes 245764
